TPU v7x, 512 devices: a whole 4x8x8 slice. The times are simulated.
512 devices in a mesh: section: 32 (over y, x_lo, core), tp: 16 (over x_hi, z).
Axes of the slice: x: 4 (x_hi: 2, x_lo: 2; x = x_hi * 2 + x_lo), y: 8, z: 8, core: 2. Of those that a mesh axis runs over, the one named last changes fastest.
Arguments:
- acts: bfloat16 [32, 768, 12288], P('section', None, 'tp'), may hold values from -6 to 6
- plan: int32 [2, 32], replicated, may hold values from 0 to 1
- norm_gain: float32 [32, 2, 12288], P('section', None, 'tp'), may hold values from 0.25 to 1.75
- query_gain: float32 [32, 2, 12288], P('section', None, 'tp'), may hold values from 0.25 to 6
- key_gain: float32 [32, 2, 12288], P('section', None, 'tp'), may hold values from 0.25 to 6
- value_gain: float32 [32, 2, 12288], P('section', None, 'tp'), may hold values from 1 to 8
Outputs:
- final_acts: bfloat16 [32, 768, 12288], P('section', None, 'tp')
- stashed: bfloat16 [32, 2, 768, 12288], P('section', None, None, 'tp')
All inputs are finite; a program needn't handle non-finite values.
Results may differ from a plain program's by a relative error of at most 0.012.
The roundings to bfloat16 on the way count: a program that leaves them out, or rounds other values in their place, can miss the bound.
Values may be sent and summed in bfloat16 or wider, within the bound.
No kernel may reach another device: no remote copies, remote signals or barrier semaphores. Data moves between devices by JAX's collectives and lax.ppermute only.
A program may use at most 64 MiB of HBM per device.

v0:
```python
import jax
import jax.numpy as jnp
from jax import lax
from jax.sharding import PartitionSpec as P

D = 12288
HEAD = 128
STEPS = 2


def swapped(array, axis, stride):
    return lax.ppermute(array, axis, [(i, i ^ 1 << stride) for i in range(lax.axis_size(axis))])


def passed_along(array, axis, by):
    size = lax.axis_size(axis)
    return lax.ppermute(array, axis, [(i, (i + by) % size) for i in range(size)])


def mixer(x, norm_g, query_g, key_g, value_g):
    xf = x.astype(jnp.float32)
    seq_len, local_width = xf.shape
    total = lax.psum(jnp.sum(xf * xf, axis=-1, keepdims=True), "tp")
    normed = xf * lax.rsqrt(total / D + 1e-05) * norm_g
    local_heads = local_width // HEAD
    query = (normed * query_g).astype(jnp.bfloat16).reshape(seq_len, local_heads, HEAD)
    keys = (normed * key_g).astype(jnp.bfloat16).reshape(seq_len, local_heads, HEAD)
    values = normed.astype(jnp.bfloat16).reshape(seq_len, local_heads, HEAD)
    scores = jnp.einsum("qhd,khd->hqk", query, keys, preferred_element_type=jnp.float32) / jnp.sqrt(
        jnp.float32(HEAD)
    )
    rows = lax.broadcasted_iota(jnp.int32, (seq_len, seq_len), 0)
    cols = lax.broadcasted_iota(jnp.int32, (seq_len, seq_len), 1)
    scores = jnp.where((cols <= rows)[None], scores, jnp.float32(-1e30))
    top = jnp.max(scores, axis=-1, keepdims=True)
    weights = jnp.exp(scores - top)
    probs = (weights / jnp.sum(weights, axis=-1, keepdims=True)).astype(jnp.bfloat16)
    att = jnp.einsum("hqk,khd->qhd", probs, values, preferred_element_type=jnp.float32).reshape(
        seq_len, local_width
    )
    return (xf + value_g * att).astype(jnp.bfloat16)


def local(acts, plan, norm_gain, query_gain, key_gain, value_gain):
    section_id = lax.axis_index("section")
    section_count = lax.axis_size("section")
    top_bit = section_count.bit_length() - 2
    current = acts
    kept = []
    for step in range(STEPS):
        kept.append(swapped(current, "section", top_bit))
        lap = lax.dynamic_index_in_dim(plan[step], section_id, 0, keepdims=False)
        norm_g = lax.dynamic_index_in_dim(norm_gain[0], lap, 0, keepdims=False)
        query_g = lax.dynamic_index_in_dim(query_gain[0], lap, 0, keepdims=False)
        key_g = lax.dynamic_index_in_dim(key_gain[0], lap, 0, keepdims=False)
        value_g = lax.dynamic_index_in_dim(value_gain[0], lap, 0, keepdims=False)
        output = mixer(current[0], norm_g, query_g, key_g, value_g)
        current = passed_along(output[None], "section", 1)
    stash = jnp.stack(kept, axis=1)
    return (current, stash)


def solution(mesh):
    return jax.shard_map(
        local,
        mesh=mesh,
        in_specs=(
            P("section", None, "tp"),
            P(),
            P("section", None, "tp"),
            P("section", None, "tp"),
            P("section", None, "tp"),
            P("section", None, "tp"),
        ),
        out_specs=(P("section", None, "tp"), P("section", None, None, "tp")),
        check_vma=False,
    )
```

profile of v0, /device:TPU:64, one launch (start us, length us, event | category | flops | bytes accessed | tf_op | source)
XLA Modules:
  0.0 230.3 jit_solution(2942149932000831390)
XLA Ops:
  0.6 0.0 copy-start.1
  0.6 0.2 iota_compare_fusion
  0.8 0.0 copy-start
  0.8 0.8 fusion.44
  1.6 0.7 constant_dynamic-slice_fusion
  6.3 0.8 dynamic-slice_reduce_fusion.1
  7.1 0.0 copy-start.5
  7.1 1.4 dynamic-slice_reduce_fusion.2
  8.5 0.0 copy-start.6
  8.5 1.6 copy.18
  10.1 0.3 multiply_reduce_fusion.1
  10.4 42.7 %psum.14 = f32[768,1]{0,1:T(1,128)S(1)} all-reduce(f32[768,1]{0,1:T(1,128)S(1)} %broadcast_in_dim.22), channel_id=1, replica_groups=mesh['section'=32,'tp'=16] {'tp'}, use_global_device_ids=true, to_apply=%region_1.2 | all-reduce | flops 768 | bytes 6144 | tf_op jit(solution)/shard_map/psum | solution.py:23
  53.1 0.0 copy-done.1
  53.1 0.6 dynamic-slice_reduce_fusion
  53.7 0.0 copy-start.7
  53.7 0.0 copy-done
  53.7 0.0 copy-done.5
  53.7 0.0 copy-done.6
  53.7 0.6 copy-done.7
  54.3 6.5 %fusion.45 = f32[6,768]{1,0:T(8,128)} fusion(pred[768,768]{0,1:T(8,128)(4,1)S(1)} %iota_compare_fusion, f32[6,128]{1,0:T(8,128)S(1)} %bitcast.41, f32[6,128]{1,0:T(8,128)S(1)} %bitcast.43, f32[768]{0:T(1024)S(1)} %rsqrt_reduce_fusion.1, f32[6,128]{1,0:T(8,128)S(1)} %bitcast.45, bf16[768,6,128]{0,2,1:T(8,128)(2,1)S(1)} %bitcast.30), kind=kOutput, calls=%fused_computation.67 | convolution fusion | flops 926024448 | bytes 1800192 | tf_op jit(solution)/shard_map/sub | solution.py:36
  60.8 0.0 copy-start.2
  60.8 8.1 %fusion.8 = f32[6,128,768]{2,1,0:T(8,128)S(1)} fusion(f32[6,768]{1,0:T(8,128)} %fusion.45, f32[6,128]{1,0:T(8,128)} %bitcast.44, f32[768]{0:T(1024)S(1)} %rsqrt_reduce_fusion.1, pred[768,768]{0,1:T(8,128)(4,1)} %copy-done, f32[6,128]{1,0:T(8,128)} %bitcast.42, f32[6,128]{1,0:T(8,128)} %bitcast.46, bf16[768,6,128]{0,2,1:T(8,128)(2,1)S(1)} %bitcast.31), kind=kOutput, calls=%fused_computation.14 | convolution fusion | flops 1837896960 | bytes 4159488 | tf_op jit(solution)/shard_map/hqk,khd->qhd/dot_general | solution.py:38
  68.9 0.0 copy-done.2
  68.9 0.0 copy-start.3
  69.0 0.0 copy-start.4
  69.0 0.3 fusion.15
  69.3 2.1 collective-permute-start
  71.4 7.7 %collective-permute-start.2 = (bf16[1,768,768]{1,2,0:T(8,128)(2,1)S(1)}, bf16[1,768,768]{1,2,0:T(8,128)(2,1)}, u32[]{:S(2)}, u32[]{:S(2)}) collective-permute-start(bf16[1,768,768]{1,2,0:T(8,128)(2,1)S(1)} %copy.18), channel_id=1, source_target_pairs={{0,256},{16,272},{32,288},{48,304},{64,320},{80,336},{96,352},{112... | collective-permute-start | bytes 3538952 | tf_op jit(solution)/shard_map/ppermute | solution.py:12
  79.2 26.5 %collective-permute-done = bf16[1,768,768]{1,2,0:T(8,128)(2,1)S(1)} collective-permute-done((bf16[1,768,768]{1,2,0:T(8,128)(2,1)S(1)}, bf16[1,768,768]{1,2,0:T(8,128)(2,1)S(1)}, u32[]{:S(2)}, u32[]{:S(2)}) %collective-permute-start) | collective-permute-done | bytes 1179680 | tf_op jit(solution)/shard_map/ppermute | solution.py:17
  105.7 0.3 multiply_reduce_fusion
  106.0 41.7 %psum.15 = f32[768,1]{0,1:T(1,128)S(1)} all-reduce(f32[768,1]{0,1:T(1,128)S(1)} %broadcast_in_dim.25), channel_id=1, replica_groups=mesh['section'=32,'tp'=16] {'tp'}, use_global_device_ids=true, to_apply=%region_5.6 | all-reduce | flops 768 | bytes 6144 | tf_op jit(solution)/shard_map/psum | solution.py:23
  147.7 0.0 copy-done.3
  147.7 0.0 copy-done.4
  147.7 6.9 %fusion.46 = f32[6,768]{1,0:T(8,128)S(1)} fusion(pred[768,768]{0,1:T(8,128)(4,1)} %copy-done, f32[6,128]{1,0:T(8,128)S(1)} %bitcast.35, f32[6,128]{1,0:T(8,128)S(1)} %bitcast.37, f32[768]{0:T(1024)S(1)} %rsqrt_reduce_fusion, f32[6,128]{1,0:T(8,128)S(1)} %bitcast.39, bf16[768,6,128]{0,2,1:T(8,128)(2,1)S(1)} %bitcast.32), kind=kOutput, calls=%fused_computation.68 | convolution fusion | flops 926024448 | bytes 1800192 | tf_op jit(solution)/shard_map/sub | solution.py:36
  154.6 9.5 %fusion.9 = f32[6,128,768]{2,1,0:T(8,128)} fusion(f32[6,768]{1,0:T(8,128)S(1)} %fusion.46, f32[6,128]{1,0:T(8,128)S(1)} %bitcast.38, f32[768]{0:T(1024)S(1)} %rsqrt_reduce_fusion, pred[768,768]{0,1:T(8,128)(4,1)} %copy-done, f32[6,128]{1,0:T(8,128)S(1)} %bitcast.36, f32[6,128]{1,0:T(8,128)S(1)} %bitcast.40, bf16[768,6,128]{0,2,1:T(8,128)(2,1)S(1)} %bitcast.33), kind=kOutput, calls=%fused_computation.15 | convolution fusion | flops 1837896960 | bytes 4159488 | tf_op jit(solution)/shard_map/hqk,khd->qhd/dot_general | solution.py:38
  164.2 41.9 %collective-permute-start.3 = (bf16[1,768,768]{1,2,0:T(8,128)(2,1)S(1)}, bf16[1,768,768]{1,2,0:T(8,128)(2,1)S(1)}, u32[]{:S(2)}, u32[]{:S(2)}) collective-permute-start(bf16[1,768,768]{1,2,0:T(8,128)(2,1)S(1)} %collective-permute-done), channel_id=1, source_target_pairs={{0,256},{16,272},{32,288},{48,304},{64,320},{80,336},{96,352},{112... | collective-permute-start | bytes 3538952 | tf_op jit(solution)/shard_map/ppermute | solution.py:12
  206.0 3.0 %fusion.13 = bf16[1,768,768]{1,2,0:T(8,128)(2,1)} fusion(f32[6,128,768]{2,1,0:T(8,128)} %fusion.9, f32[768]{0:T(1024)S(1)} %get-tuple-element.4, bf16[1,768,768]{1,2,0:T(8,128)(2,1)S(1)} %collective-permute-done), kind=kLoop, calls=%fused_computation.21 | loop fusion | flops 2359296 | bytes 4721664 | tf_op jit(solution)/shard_map/convert_element_type | solution.py:41
  209.0 1.9 collective-permute-start.1
  211.0 0.0 collective-permute-done.2
  211.0 9.3 %collective-permute-done.3 = bf16[1,768,768]{1,2,0:T(8,128)(2,1)S(1)} collective-permute-done((bf16[1,768,768]{1,2,0:T(8,128)(2,1)S(1)}, bf16[1,768,768]{1,2,0:T(8,128)(2,1)S(1)}, u32[]{:S(2)}, u32[]{:S(2)}) %collective-permute-start.3) | collective-permute-done | bytes 1179680 | tf_op jit(solution)/shard_map/ppermute | solution.py:12
  220.3 1.5 pad_maximum_fusion
  221.8 2.4 %copy.27 = bf16[1,2,768,768]{3,2,1,0:T(8,128)(2,1)} copy(bf16[1,2,768,768]{2,3,1,0:T(8,128)(2,1)S(1)} %pad_maximum_fusion) | data formatting | bytes 4718592
  224.2 4.7 %collective-permute-done.1 = bf16[1,768,768]{1,2,0:T(8,128)(2,1)S(1)} collective-permute-done((bf16[1,768,768]{1,2,0:T(8,128)(2,1)}, bf16[1,768,768]{1,2,0:T(8,128)(2,1)S(1)}, u32[]{:S(2)}, u32[]{:S(2)}) %collective-permute-start.1) | collective-permute-done | bytes 1179680 | tf_op jit(solution)/shard_map/ppermute | solution.py:17
  228.9 1.4 copy.26
  (5 shorter events, 0.1 us)
Async XLA Ops:
  0.6 52.5 %copy-start.1 = (f32[1,2,768]{2,1,0:T(2,128)S(1)}, f32[1,2,768]{2,1,0:T(2,128)}, u32[]{:S(2)}) copy-start(f32[1,2,768]{2,1,0:T(2,128)} %param.10) | copy-start | bytes 18436
  0.8 52.9 %copy-start = (pred[768,768]{0,1:T(8,128)(4,1)}, pred[768,768]{0,1:T(8,128)(4,1)S(1)}, u32[]{:S(2)}) copy-start(pred[768,768]{0,1:T(8,128)(4,1)S(1)} %iota_compare_fusion) | copy-start | bytes 1769476
  7.1 46.6 %copy-start.5 = (f32[768]{0:T(1024)}, f32[768]{0:T(1024)S(1)}, u32[]{:S(2)}) copy-start(f32[768]{0:T(1024)S(1)} %get-tuple-element.11) | copy-start | bytes 9220
  8.5 45.2 %copy-start.6 = (f32[768]{0:T(1024)}, f32[768]{0:T(1024)S(1)}, u32[]{:S(2)}) copy-start(f32[768]{0:T(1024)S(1)} %get-tuple-element.9) | copy-start | bytes 9220
  53.7 0.6 copy-start.7
  60.8 8.1 %copy-start.2 = (f32[1,2,768]{2,1,0:T(2,128)S(1)}, f32[1,2,768]{2,1,0:T(2,128)}, u32[]{:S(2)}) copy-start(f32[1,2,768]{2,1,0:T(2,128)} %param.11) | copy-start | bytes 18436
  68.9 78.8 %copy-start.3 = (f32[768]{0:T(1024)S(1)}, f32[768]{0:T(1024)}, u32[]{:S(2)}) copy-start(f32[768]{0:T(1024)} %get-tuple-element.8) | copy-start | bytes 9220
  69.0 78.8 %copy-start.4 = (f32[768]{0:T(1024)S(1)}, f32[768]{0:T(1024)}, u32[]{:S(2)}) copy-start(f32[768]{0:T(1024)} %get-tuple-element.6) | copy-start | bytes 9220
  69.3 36.4 %collective-permute-start = (bf16[1,768,768]{1,2,0:T(8,128)(2,1)S(1)}, bf16[1,768,768]{1,2,0:T(8,128)(2,1)S(1)}, u32[]{:S(2)}, u32[]{:S(2)}) collective-permute-start(bf16[1,768,768]{1,2,0:T(8,128)(2,1)S(1)} %fusion.15), channel_id=1, source_target_pairs={{0,16},{16,32},{32,48},{48,64},{64,80},{80,96},{96,112},{112,128},... | collective-permute-start | bytes 3538952 | tf_op jit(solution)/shard_map/ppermute | solution.py:17
  71.4 139.6 %collective-permute-start.2 = (bf16[1,768,768]{1,2,0:T(8,128)(2,1)S(1)}, bf16[1,768,768]{1,2,0:T(8,128)(2,1)}, u32[]{:S(2)}, u32[]{:S(2)}) collective-permute-start(bf16[1,768,768]{1,2,0:T(8,128)(2,1)S(1)} %copy.18), channel_id=1, source_target_pairs={{0,256},{16,272},{32,288},{48,304},{64,320},{80,336},{96,352},{112... | collective-permute-start | bytes 3538952 | tf_op jit(solution)/shard_map/ppermute | solution.py:12
  164.2 56.1 %collective-permute-start.3 = (bf16[1,768,768]{1,2,0:T(8,128)(2,1)S(1)}, bf16[1,768,768]{1,2,0:T(8,128)(2,1)S(1)}, u32[]{:S(2)}, u32[]{:S(2)}) collective-permute-start(bf16[1,768,768]{1,2,0:T(8,128)(2,1)S(1)} %collective-permute-done), channel_id=1, source_target_pairs={{0,256},{16,272},{32,288},{48,304},{64,320},{80,336},{96,352},{112... | collective-permute-start | bytes 3538952 | tf_op jit(solution)/shard_map/ppermute | solution.py:12
  209.0 19.8 %collective-permute-start.1 = (bf16[1,768,768]{1,2,0:T(8,128)(2,1)}, bf16[1,768,768]{1,2,0:T(8,128)(2,1)S(1)}, u32[]{:S(2)}, u32[]{:S(2)}) collective-permute-start(bf16[1,768,768]{1,2,0:T(8,128)(2,1)} %fusion.13), channel_id=1, source_target_pairs={{0,16},{16,32},{32,48},{48,64},{64,80},{80,96},{96,112},{112,128},... | collective-permute-start | bytes 3538952 | tf_op jit(solution)/shard_map/ppermute | solution.py:17
where the time goes:
time: 231 us; the launch traced here: 230 us
  blocking collectives  84.4 us (37%)
  starting transfers between devices  53.6 us (23%)
  waiting for transfers between devices  40.5 us (18%)
  matrix products  31 us (13%)
  local copies, waits for them, and re-layouts  10.3 us (4%)
  other arithmetic  5.64 us (2%)
  between operations  4.83 us (2%)
    psum x2, blocking collectives, mixer(): total = lax.psum(jnp.sum(xf * xf, axis=-1, keepdims=True), 'tp')  84.4 us
    ppermute x2, starting transfers between devices, swapped(): lax.ppermute(array, axis, [(i, i ^ 1 << stride) for i in range(lax.axis_s...  49.6 us
    ppermute x2, waiting for transfers between devices, passed_along(): lax.ppermute(array, axis, [(i, (i + by) % size) for i in range(size)])  31.2 us
    dot_general x2, matrix products, mixer(): jnp.einsum('hqk,khd->qhd', probs, values, preferred_element_type=jnp.floa...  17.6 us
    sub x2, matrix products, mixer(): weights = jnp.exp(scores - top)  13.4 us
    ppermute x2, waiting for transfers between devices, swapped(): lax.ppermute(array, axis, [(i, i ^ 1 << stride) for i in range(lax.axis_s...  9.32 us
    unnamed x19, local copies, waits for them, and re-layouts  6.05 us
  transfers between devices with their start and end apart: 4, of which 3 were waited for; matrix products, arithmetic and copies ran while one was open for 10% of the time, Pallas kernels for 0%

commit v1 on v0

v1 whole, which is shorter than its diff:
```python
import functools
import math

import jax
import jax.numpy as jnp
from jax import lax
from jax.experimental import pallas as pl
from jax.experimental.pallas import tpu as pltpu
from jax.sharding import Mesh
from jax.sharding import PartitionSpec as P

D = 12288
HEAD = 128
BLOCK = 256
EPS = 1e-05
ACROSS_LAST = (((1,), (1,)), ((), ()))


def square_sums(y):
    yf = y.astype(jnp.float32)
    squared = yf * yf
    high = squared.astype(jnp.bfloat16)
    low = (squared - high.astype(jnp.float32)).astype(jnp.bfloat16)
    ones = jnp.ones((8, y.shape[1]), jnp.bfloat16)
    return lax.dot_general(ones, high, ACROSS_LAST, preferred_element_type=jnp.float32) + lax.dot_general(
        ones, low, ACROSS_LAST, preferred_element_type=jnp.float32
    )


def first_kernel(lap_ref, norm_ref, query_ref, key_ref, value_ref, x_ref, now_ref, later_ref):
    sums = square_sums(x_ref[...])
    rows = [[], []]
    for step in range(2):
        for gain in (norm_ref, query_ref, key_ref, value_ref):
            rows[step].append(jnp.where(lap_ref[step] == 0, gain[0:1], gain[1:2]))
    now_ref[...] = jnp.concatenate([sums[0:1]] + rows[0] + [sums[1:4]], axis=0)
    later_ref[...] = jnp.concatenate([sums[0:1]] + rows[1] + [sums[1:4]], axis=0)


def first(laps, gains, x):
    shape = jax.ShapeDtypeStruct((8, x.shape[1]), jnp.float32)
    return pl.pallas_call(
        first_kernel,
        in_specs=[pl.BlockSpec(memory_space=pltpu.SMEM)] + [pl.BlockSpec(memory_space=pltpu.VMEM)] * 5,
        out_shape=(shape, shape),
        compiler_params=pltpu.CompilerParams(vmem_limit_bytes=24 * 2**20),
    )(laps, *gains, x)


def mixer_kernel(with_sums, total_row, total_ref, gain_ref, x_ref, y_ref, *rest):
    seq, width = x_ref.shape
    scale = lax.rsqrt(total_ref[total_row : total_row + 1] / D + EPS)
    scale = jnp.transpose(jnp.broadcast_to(scale, (8, seq)))[:, 0:1]
    factor = math.log2(math.e) / math.sqrt(HEAD)
    causal = lax.broadcasted_iota(jnp.int32, (BLOCK, BLOCK), 1) <= lax.broadcasted_iota(
        jnp.int32, (BLOCK, BLOCK), 0
    )

    def prepare(head):
        cols = slice(head * HEAD, (head + 1) * HEAD)
        normed = x_ref[:, cols].astype(jnp.float32) * scale * gain_ref[1:2, cols]
        query = (normed * gain_ref[2:3, cols]).astype(jnp.bfloat16)
        keys = (normed * gain_ref[3:4, cols]).astype(jnp.bfloat16)
        return query, keys, normed.astype(jnp.bfloat16), cols

    def score(parts, block):
        query, keys, _, _ = parts
        lo, hi = block * BLOCK, (block + 1) * BLOCK
        raw = lax.dot_general(query[lo:hi], keys[:hi], ACROSS_LAST, preferred_element_type=jnp.float32)
        last = jnp.where(causal, raw[:, lo:], -1e30)
        return jnp.concatenate([raw[:, :lo], last], axis=1) if lo else last

    def softmax(raw):
        top = jnp.max(raw, axis=1, keepdims=True)
        weights = jnp.exp2((raw - top) * factor)
        return (weights * (1.0 / jnp.sum(weights, axis=1, keepdims=True))).astype(jnp.bfloat16)

    def finish(parts, block, probs):
        _, _, values, cols = parts
        lo, hi = block * BLOCK, (block + 1) * BLOCK
        att = jnp.dot(probs, values[:hi], preferred_element_type=jnp.float32)
        y_ref[lo:hi, cols] = (x_ref[lo:hi, cols].astype(jnp.float32) + gain_ref[4:5, cols] * att).astype(jnp.bfloat16)

    tasks = [(head, block) for head in range(width // HEAD) for block in range(seq // BLOCK)]
    ready = {}
    scores = {}

    def issue(at):
        head, block = tasks[at]
        if head not in ready:
            ready[head] = prepare(head)
        scores[at] = score(ready[head], block)

    issue(0)
    pending = None
    for at, (head, block) in enumerate(tasks):
        if at + 1 < len(tasks):
            issue(at + 1)
        probs = softmax(scores.pop(at))
        if pending is not None:
            finish(*pending)
        pending = (ready[head], block, probs)
    finish(*pending)
    if with_sums:
        rest[0][...] = square_sums(y_ref[...])


def mixer(x, total, row, gains, first_head=0, with_sums=False):
    seq, width = x.shape
    out_shape = [jax.ShapeDtypeStruct(x.shape, jnp.bfloat16)]
    out_specs = [pl.BlockSpec((seq, width), lambda i: (0, 0))]
    if with_sums:
        out_shape.append(jax.ShapeDtypeStruct((8, seq), jnp.float32))
        out_specs.append(pl.BlockSpec((8, seq), lambda i: (0, 0)))
    at = first_head * HEAD // width
    out = pl.pallas_call(
        functools.partial(mixer_kernel, with_sums, row),
        grid=(1,),
        in_specs=[
            pl.BlockSpec(total.shape, lambda i: (0, 0)),
            pl.BlockSpec((8, width), lambda i: (0, at)),
            pl.BlockSpec((seq, width), lambda i: (0, 0)),
        ],
        out_specs=out_specs,
        out_shape=out_shape,
        compiler_params=pltpu.CompilerParams(vmem_limit_bytes=32 * 2**20),
        cost_estimate=pl.CostEstimate(
            flops=12 * seq * seq * width, bytes_accessed=4 * seq * width, transcendentals=seq * seq * width // HEAD
        ),
    )(total, gains, x)
    return out if with_sums else out[0]


def moved(array, by):
    size = lax.axis_size("section")
    return lax.ppermute(array, "section", [(i, (i + by) % size) for i in range(size)])


def summed(part):
    size = lax.axis_size("z")
    copies = lax.all_to_all(jnp.broadcast_to(part[None], (size,) + part.shape), "z", 0, 0, tiled=True)
    return lax.psum(copies.sum(0), "xh")


def local(acts, plan, norm_gain, query_gain, key_gain, value_gain):
    half = lax.axis_size("section") // 2
    x = acts[0]
    width = x.shape[1] // 2
    laps = lax.dynamic_index_in_dim(plan, lax.axis_index("section"), 1, keepdims=False)
    now, later = first(laps, (norm_gain[0], query_gain[0], key_gain[0], value_gain[0]), x)
    gains_now = moved(now, 2)
    gains_mirror = moved(now, half)
    behind = moved(x, 2)
    mirror = [moved(x[:, i * width : (i + 1) * width], half) for i in range(2)]
    gains_later = moved(later, 1)

    totals = summed(jnp.concatenate([gains_now[0:1], gains_mirror[0:1]], axis=0))
    once, sums = mixer(behind, totals, 0, gains_now, with_sums=True)
    totals_later = summed(sums[0:1])
    early, totals_later = lax.optimization_barrier((mirror[0], totals_later))
    mixed = [mixer(early, totals, 1, gains_mirror)]
    twice = mixer(once, totals_later, 0, gains_later)
    late, twice = lax.optimization_barrier((mirror[1], twice))
    mixed.append(mixer(late, totals, 1, gains_mirror, first_head=width // HEAD))
    relayed = [moved(part, 1) for part in mixed]
    stash = jnp.stack([jnp.concatenate(mirror, axis=1), jnp.concatenate(relayed, axis=1)], axis=0)
    return (twice[None], stash[None])


def solution(mesh):
    sections, shards = mesh.shape["section"], mesh.shape["tp"]
    fine = Mesh(mesh.devices.reshape(sections, 2, shards // 2), ("section", "xh", "z"))
    tp = ("xh", "z")
    gain = P("section", None, tp)
    return jax.shard_map(
        local,
        mesh=fine,
        in_specs=(P("section", None, tp), P(), gain, gain, gain, gain),
        out_specs=(P("section", None, tp), P("section", None, None, tp)),
        check_vma=False,
    )
```

time: 231 us -> 135 us (0.58)
  the two profiles are of different devices: /device:TPU:64 before, /device:TPU:4 now
where the time goes in v1:
time: 135 us; the launch traced here: 134 us
  starting transfers between devices  47.2 us (35%)
  waiting for transfers between devices  44.5 us (33%)
  Pallas kernels  17.5 us (13%)
  blocking collectives  13.2 us (10%)
  local copies, waits for them, and re-layouts  8.77 us (6%)
  other arithmetic  1.87 us (1%)
    ppermute x8, waiting for transfers between devices, moved(): lax.ppermute(array, 'section', [(i, (i + by) % size) for i in range(size)])  38.6 us
    ppermute x8, starting transfers between devices, moved(): lax.ppermute(array, 'section', [(i, (i + by) % size) for i in range(size)])  29.6 us
    all_to_all x2, starting transfers between devices, summed(): lax.all_to_all(jnp.broadcast_to(part[None], (size,) + part.shape), 'z', 0...  17.5 us
    pallas_call x4, Pallas kernels, mixer(): pl.pallas_call(functools.partial(mixer_kernel, with_sums, row), grid=(1,)...  16.2 us
    psum x2, blocking collectives, summed(): return lax.psum(copies.sum(0), 'xh')  13.2 us
    unnamed x18, local copies, waits for them, and re-layouts  6.37 us
    all_to_all x2, waiting for transfers between devices, summed(): lax.all_to_all(jnp.broadcast_to(part[None], (size,) + part.shape), 'z', 0...  5.9 us
  transfers between devices with their start and end apart: 10, of which 6 were waited for; matrix products, arithmetic and copies ran while one was open for 2% of the time, Pallas kernels for 11%

profile of v1, /device:TPU:4, one launch (start us, length us, event | category | flops | bytes accessed | tf_op | source)
XLA Modules:
  0.0 133.8 jit_solution(14637972385490792624)
XLA Ops:
  0.6 0.0 copy-start
  0.6 3.1 %collective-permute-start.4 = (bf16[768,768]{1,0:T(8,128)(2,1)}, bf16[768,768]{1,0:T(8,128)(2,1)S(1)}, u32[]{:S(2)}, u32[]{:S(2)}) collective-permute-start(bf16[768,768]{1,0:T(8,128)(2,1)} %bitcast.12), channel_id=1, source_target_pairs={{0,32},{16,48},{32,64},{48,80},{64,96},{80,112},{96,128},{112,144}... | collective-permute-start | bytes 3538952 | tf_op jit(solution)/shard_map/ppermute | solution.py:136
  3.8 0.0 copy-done
  3.8 0.2 dynamic-slice_reduce_fusion.lap_ref
  4.0 1.3 copy-done.1
  5.2 0.0 copy-start.3
  5.2 0.7 copy-done.3
  5.9 0.0 copy-start.4
  5.9 0.7 copy-done.4
  6.6 0.0 copy-start.5
  6.6 0.7 copy-done.5
  7.3 0.7 copy-done.6
  8.0 0.0 copy-start.2
  8.0 1.3 shard_map.77
  9.3 7.7 %collective-permute-start.3 = (f32[8,768]{1,0:T(8,128)S(1)}, f32[8,768]{1,0:T(8,128)S(1)}, u32[]{:S(2)}, u32[]{:S(2)}) collective-permute-start(f32[8,768]{1,0:T(8,128)S(1)} %get-tuple-element.10), channel_id=1, source_target_pairs={{0,256},{16,272},{32,288},{48,304},{64,320},{80,336},{96,352},{112... | collective-permute-start | bytes 73736 | tf_op jit(solution)/shard_map/ppermute | solution.py:136
  17.1 2.9 %collective-permute-start.2 = (f32[8,768]{1,0:T(8,128)S(1)}, f32[8,768]{1,0:T(8,128)S(1)}, u32[]{:S(2)}, u32[]{:S(2)}) collective-permute-start(f32[8,768]{1,0:T(8,128)S(1)} %get-tuple-element.10), channel_id=1, source_target_pairs={{0,32},{16,48},{32,64},{48,80},{64,96},{80,112},{96,128},{112,144}... | collective-permute-start | bytes 73736 | tf_op jit(solution)/shard_map/ppermute | solution.py:136
  19.9 0.0 collective-permute-done.3.gain_ref
  19.9 13.6 %collective-permute-done.2.gain_ref = f32[8,768]{1,0:T(8,128)S(1)} collective-permute-done((f32[8,768]{1,0:T(8,128)S(1)}, f32[8,768]{1,0:T(8,128)S(1)}, u32[]{:S(2)}, u32[]{:S(2)}) %collective-permute-start.2) | collective-permute-done | bytes 24608 | tf_op jit(solution)/shard_map/ppermute | solution.py:136
  33.6 0.6 broadcast_in_dim.20
  34.2 10.3 %all-to-all-start = ((f32[8,2,768]{2,1,0:T(2,128)}), f32[8,2,768]{2,1,0:T(2,128)S(1)}, u32[]{:S(2)}, u32[]{:S(2)}) async-start(f32[8,2,768]{2,1,0:T(2,128)} %broadcast_in_dim.20), calls=%async_computation | async-start | bytes 98304 | tf_op jit(solution)/shard_map/all_to_all | solution.py:141
  44.6 0.0 copy-done.2
  44.6 0.9 fusion
  45.5 8.3 %collective-permute-start.1 = (bf16[768,384]{1,0:T(8,128)(2,1)}, bf16[768,384]{1,0:T(8,128)(2,1)S(1)}, u32[]{:S(2)}, u32[]{:S(2)}) collective-permute-start(bf16[768,384]{1,0:T(8,128)(2,1)} %get-tuple-element.18), channel_id=1, source_target_pairs={{0,256},{16,272},{32,288},{48,304},{64,320},{80,336},{96,352},{112... | collective-permute-start | bytes 1769480 | tf_op jit(solution)/shard_map/ppermute | solution.py:136
  53.8 1.9 %collective-permute-start = (bf16[768,384]{1,0:T(8,128)(2,1)S(1)}, bf16[768,384]{1,0:T(8,128)(2,1)S(1)}, u32[]{:S(2)}, u32[]{:S(2)}) collective-permute-start(bf16[768,384]{1,0:T(8,128)(2,1)S(1)} %get-tuple-element.19), channel_id=1, source_target_pairs={{0,256},{16,272},{32,288},{48,304},{64,320},{80,336},{96,352},{112... | collective-permute-start | bytes 1769480 | tf_op jit(solution)/shard_map/ppermute | solution.py:136
  55.7 0.0 all-to-all-done
  55.8 6.5 %psum.14.total_ref = f32[2,768]{1,0:T(2,128)S(1)} all-reduce(f32[2,768]{1,0:T(2,128)S(1)} %reduce_sum.20), channel_id=1, replica_groups=mesh['section'=32,'xh'=2,'z'=8] {'xh'}, use_global_device_ids=true, to_apply=%region_1.2 | all-reduce | flops 1536 | bytes 12288 | tf_op jit(solution)/shard_map/psum | solution.py:142
  62.3 0.0 collective-permute-done.4.x_ref
  62.3 5.4 %shard_map.78 = (bf16[768,768]{1,0:T(8,128)(2,1)S(1)}, f32[8,768]{1,0:T(8,128)S(1)}) custom-call(f32[2,768]{1,0:T(2,128)S(1)} %psum.14.total_ref, f32[8,768]{1,0:T(8,128)S(1)} %collective-permute-done.2.gain_ref, bf16[768,768]{1,0:T(8,128)(2,1)S(1)} %collective-permute-done.4.x_ref), custom_call_target="tpu_custom_call" | custom-call | flops 5435817984 | bytes 2359296 | tf_op jit(solution)/shard_map/pallas_call | solution.py:116
  67.7 1.0 copy-done.7
  68.7 0.6 broadcast_in_dim.22
  69.4 7.2 %all-to-all-start.1 = ((f32[8,1,768]{2,1,0:T(1,128)}), f32[8,1,768]{2,1,0:T(1,128)S(1)}, u32[]{:S(2)}, u32[]{:S(2)}) async-start(f32[8,1,768]{2,1,0:T(1,128)} %broadcast_in_dim.22), calls=%async_computation.1 | async-start | bytes 49152 | tf_op jit(solution)/shard_map/all_to_all | solution.py:141
  76.6 1.9 %collective-permute-start.5 = (f32[8,768]{1,0:T(8,128)S(1)}, f32[8,768]{1,0:T(8,128)S(1)}, u32[]{:S(2)}, u32[]{:S(2)}) collective-permute-start(f32[8,768]{1,0:T(8,128)S(1)} %get-tuple-element.13), channel_id=1, source_target_pairs={{0,16},{16,32},{32,48},{48,64},{64,80},{80,96},{96,112},{112,128},... | collective-permute-start | bytes 73736 | tf_op jit(solution)/shard_map/ppermute | solution.py:136
  78.5 5.9 %all-to-all-done.1 = f32[8,1,768]{2,1,0:T(1,128)S(1)} async-done(((f32[8,1,768]{2,1,0:T(1,128)}), f32[8,1,768]{2,1,0:T(1,128)S(1)}, u32[]{:S(2)}, u32[]{:S(2)}) %all-to-all-start.1) | async-done | bytes 24608 | tf_op jit(solution)/shard_map/all_to_all | solution.py:141
  84.4 6.6 %psum.15.total_ref = f32[1,768]{1,0:T(1,128)S(1)} all-reduce(f32[1,768]{1,0:T(1,128)S(1)} %reduce_sum.22), channel_id=1, replica_groups=mesh['section'=32,'xh'=2,'z'=8] {'xh'}, use_global_device_ids=true, to_apply=%region_3.4 | all-reduce | flops 768 | bytes 6144 | tf_op jit(solution)/shard_map/psum | solution.py:142
  91.1 2.0 %collective-permute-done.1.x_ref = bf16[768,384]{1,0:T(8,128)(2,1)S(1)} collective-permute-done((bf16[768,384]{1,0:T(8,128)(2,1)}, bf16[768,384]{1,0:T(8,128)(2,1)S(1)}, u32[]{:S(2)}, u32[]{:S(2)}) %collective-permute-start.1) | collective-permute-done | bytes 589856 | tf_op jit(solution)/shard_map/ppermute | solution.py:136
  93.1 9.9 %collective-permute-done.5.gain_ref = f32[8,768]{1,0:T(8,128)S(1)} collective-permute-done((f32[8,768]{1,0:T(8,128)S(1)}, f32[8,768]{1,0:T(8,128)S(1)}, u32[]{:S(2)}, u32[]{:S(2)}) %collective-permute-start.5) | collective-permute-done | bytes 24608 | tf_op jit(solution)/shard_map/ppermute | solution.py:136
  103.0 1.3 copy-done.8
  104.2 5.6 %shard_map.79 = bf16[768,768]{1,0:T(8,128)(2,1)} custom-call(f32[1,768]{1,0:T(1,128)S(1)} %psum.15.total_ref, f32[8,768]{1,0:T(8,128)S(1)} %collective-permute-done.5.gain_ref, bf16[768,768]{1,0:T(8,128)(2,1)S(1)} %copy-done.8), custom_call_target="tpu_custom_call" | custom-call | flops 5435817984 | bytes 2359296 | tf_op jit(solution)/shard_map/pallas_call | solution.py:116
  109.8 0.0 collective-permute-done.x_ref
  109.8 2.6 %shard_map.80 = bf16[768,384]{1,0:T(8,128)(2,1)S(1)} custom-call(f32[2,768]{1,0:T(2,128)S(1)} %psum.14.total_ref, f32[8,768]{1,0:T(8,128)S(1)} %collective-permute-done.3.gain_ref, bf16[768,384]{1,0:T(8,128)(2,1)S(1)} %collective-permute-done.1.x_ref), custom_call_target="tpu_custom_call" | custom-call | flops 2717908992 | bytes 1179648 | tf_op jit(solution)/shard_map/pallas_call | solution.py:116
  112.5 1.9 %collective-permute-start.6 = (bf16[768,384]{1,0:T(8,128)(2,1)S(1)}, bf16[768,384]{1,0:T(8,128)(2,1)S(1)}, u32[]{:S(2)}, u32[]{:S(2)}) collective-permute-start(bf16[768,384]{1,0:T(8,128)(2,1)S(1)} %shard_map.80), channel_id=1, source_target_pairs={{0,16},{16,32},{32,48},{48,64},{64,80},{80,96},{96,112},{112,128},... | collective-permute-start | bytes 1769480 | tf_op jit(solution)/shard_map/ppermute | solution.py:136
  114.4 2.6 %shard_map.81 = bf16[768,384]{1,0:T(8,128)(2,1)S(1)} custom-call(f32[2,768]{1,0:T(2,128)S(1)} %psum.14.total_ref, f32[8,768]{1,0:T(8,128)S(1)} %collective-permute-done.3.gain_ref, bf16[768,384]{1,0:T(8,128)(2,1)S(1)} %collective-permute-done.x_ref), custom_call_target="tpu_custom_call" | custom-call | flops 2717908992 | bytes 1179648 | tf_op jit(solution)/shard_map/pallas_call | solution.py:116
  117.0 1.9 %collective-permute-start.7 = (bf16[768,384]{1,0:T(8,128)(2,1)S(1)}, bf16[768,384]{1,0:T(8,128)(2,1)S(1)}, u32[]{:S(2)}, u32[]{:S(2)}) collective-permute-start(bf16[768,384]{1,0:T(8,128)(2,1)S(1)} %shard_map.81), channel_id=1, source_target_pairs={{0,16},{16,32},{32,48},{48,64},{64,80},{80,96},{96,112},{112,128},... | collective-permute-start | bytes 1769480 | tf_op jit(solution)/shard_map/ppermute | solution.py:136
  118.9 0.1 maximum_bitcast_fusion.1
  119.0 6.7 %collective-permute-done.6 = bf16[768,384]{1,0:T(8,128)(2,1)S(1)} collective-permute-done((bf16[768,384]{1,0:T(8,128)(2,1)S(1)}, bf16[768,384]{1,0:T(8,128)(2,1)S(1)}, u32[]{:S(2)}, u32[]{:S(2)}) %collective-permute-start.6) | collective-permute-done | bytes 589856 | tf_op jit(solution)/shard_map/ppermute | solution.py:136
  125.8 6.3 %collective-permute-done.7 = bf16[768,384]{1,0:T(8,128)(2,1)S(1)} collective-permute-done((bf16[768,384]{1,0:T(8,128)(2,1)S(1)}, bf16[768,384]{1,0:T(8,128)(2,1)S(1)}, u32[]{:S(2)}, u32[]{:S(2)}) %collective-permute-start.7) | collective-permute-done | bytes 589856 | tf_op jit(solution)/shard_map/ppermute | solution.py:136
  132.1 0.1 maximum_bitcast_fusion.2
  132.2 1.6 %maximum_bitcast_fusion = bf16[1,2,768,768]{3,2,1,0:T(8,128)(2,1)} fusion(bf16[1,768,768]{2,1,0:T(8,128)(2,1)S(1)} %maximum_bitcast_fusion.2, bf16[1,768,768]{2,1,0:T(8,128)(2,1)S(1)} %maximum_bitcast_fusion.1), kind=kLoop, calls=%fused_computation | loop fusion | flops 1179648 | bytes 4718592 | tf_op jit(solution)/shard_map/broadcast_in_dim | solution.py:167
  (11 shorter events, 0.1 us)
Async XLA Ops:
  0.6 3.1 %copy-start = (s32[2,32]{1,0:T(2,128)S(1)}, s32[2,32]{1,0:T(2,128)}, u32[]{:S(2)}) copy-start(s32[2,32]{1,0:T(2,128)} %param.7) | copy-start | bytes 772
  0.6 61.6 %collective-permute-start.4 = (bf16[768,768]{1,0:T(8,128)(2,1)}, bf16[768,768]{1,0:T(8,128)(2,1)S(1)}, u32[]{:S(2)}, u32[]{:S(2)}) collective-permute-start(bf16[768,768]{1,0:T(8,128)(2,1)} %bitcast.12), channel_id=1, source_target_pairs={{0,32},{16,48},{32,64},{48,80},{64,96},{80,112},{96,128},{112,144}... | collective-permute-start | bytes 3538952 | tf_op jit(solution)/shard_map/ppermute | solution.py:136
  4.0 1.3 copy-start.1
  5.2 0.7 copy-start.3
  5.9 0.7 copy-start.4
  6.6 0.7 copy-start.5
  7.3 0.7 copy-start.6
  8.0 36.6 %copy-start.2 = (bf16[1,768,768]{2,1,0:T(8,128)(2,1)S(1)}, bf16[1,768,768]{2,1,0:T(8,128)(2,1)}, u32[]{:S(2)}) copy-start(bf16[1,768,768]{2,1,0:T(8,128)(2,1)} %param.6) | copy-start | bytes 3538948
  9.3 10.6 %collective-permute-start.3 = (f32[8,768]{1,0:T(8,128)S(1)}, f32[8,768]{1,0:T(8,128)S(1)}, u32[]{:S(2)}, u32[]{:S(2)}) collective-permute-start(f32[8,768]{1,0:T(8,128)S(1)} %get-tuple-element.10), channel_id=1, source_target_pairs={{0,256},{16,272},{32,288},{48,304},{64,320},{80,336},{96,352},{112... | collective-permute-start | bytes 73736 | tf_op jit(solution)/shard_map/ppermute | solution.py:136
  17.1 16.5 %collective-permute-start.2 = (f32[8,768]{1,0:T(8,128)S(1)}, f32[8,768]{1,0:T(8,128)S(1)}, u32[]{:S(2)}, u32[]{:S(2)}) collective-permute-start(f32[8,768]{1,0:T(8,128)S(1)} %get-tuple-element.10), channel_id=1, source_target_pairs={{0,32},{16,48},{32,64},{48,80},{64,96},{80,112},{96,128},{112,144}... | collective-permute-start | bytes 73736 | tf_op jit(solution)/shard_map/ppermute | solution.py:136
  34.2 21.5 %all-to-all-start = ((f32[8,2,768]{2,1,0:T(2,128)}), f32[8,2,768]{2,1,0:T(2,128)S(1)}, u32[]{:S(2)}, u32[]{:S(2)}) async-start(f32[8,2,768]{2,1,0:T(2,128)} %broadcast_in_dim.20), calls=%async_computation | async-start | bytes 98304 | tf_op jit(solution)/shard_map/all_to_all | solution.py:141
  45.5 47.6 %collective-permute-start.1 = (bf16[768,384]{1,0:T(8,128)(2,1)}, bf16[768,384]{1,0:T(8,128)(2,1)S(1)}, u32[]{:S(2)}, u32[]{:S(2)}) collective-permute-start(bf16[768,384]{1,0:T(8,128)(2,1)} %get-tuple-element.18), channel_id=1, source_target_pairs={{0,256},{16,272},{32,288},{48,304},{64,320},{80,336},{96,352},{112... | collective-permute-start | bytes 1769480 | tf_op jit(solution)/shard_map/ppermute | solution.py:136
  53.8 56.1 %collective-permute-start = (bf16[768,384]{1,0:T(8,128)(2,1)S(1)}, bf16[768,384]{1,0:T(8,128)(2,1)S(1)}, u32[]{:S(2)}, u32[]{:S(2)}) collective-permute-start(bf16[768,384]{1,0:T(8,128)(2,1)S(1)} %get-tuple-element.19), channel_id=1, source_target_pairs={{0,256},{16,272},{32,288},{48,304},{64,320},{80,336},{96,352},{112... | collective-permute-start | bytes 1769480 | tf_op jit(solution)/shard_map/ppermute | solution.py:136
  67.7 1.1 copy-start.7
  69.4 15.0 %all-to-all-start.1 = ((f32[8,1,768]{2,1,0:T(1,128)}), f32[8,1,768]{2,1,0:T(1,128)S(1)}, u32[]{:S(2)}, u32[]{:S(2)}) async-start(f32[8,1,768]{2,1,0:T(1,128)} %broadcast_in_dim.22), calls=%async_computation.1 | async-start | bytes 49152 | tf_op jit(solution)/shard_map/all_to_all | solution.py:141
  76.6 26.4 %collective-permute-start.5 = (f32[8,768]{1,0:T(8,128)S(1)}, f32[8,768]{1,0:T(8,128)S(1)}, u32[]{:S(2)}, u32[]{:S(2)}) collective-permute-start(f32[8,768]{1,0:T(8,128)S(1)} %get-tuple-element.13), channel_id=1, source_target_pairs={{0,16},{16,32},{32,48},{48,64},{64,80},{80,96},{96,112},{112,128},... | collective-permute-start | bytes 73736 | tf_op jit(solution)/shard_map/ppermute | solution.py:136
  103.0 1.3 copy-start.8
  112.5 13.3 %collective-permute-start.6 = (bf16[768,384]{1,0:T(8,128)(2,1)S(1)}, bf16[768,384]{1,0:T(8,128)(2,1)S(1)}, u32[]{:S(2)}, u32[]{:S(2)}) collective-permute-start(bf16[768,384]{1,0:T(8,128)(2,1)S(1)} %shard_map.80), channel_id=1, source_target_pairs={{0,16},{16,32},{32,48},{48,64},{64,80},{80,96},{96,112},{112,128},... | collective-permute-start | bytes 1769480 | tf_op jit(solution)/shard_map/ppermute | solution.py:136
  117.0 15.1 %collective-permute-start.7 = (bf16[768,384]{1,0:T(8,128)(2,1)S(1)}, bf16[768,384]{1,0:T(8,128)(2,1)S(1)}, u32[]{:S(2)}, u32[]{:S(2)}) collective-permute-start(bf16[768,384]{1,0:T(8,128)(2,1)S(1)} %shard_map.81), channel_id=1, source_target_pairs={{0,16},{16,32},{32,48},{48,64},{64,80},{80,96},{96,112},{112,128},... | collective-permute-start | bytes 1769480 | tf_op jit(solution)/shard_map/ppermute | solution.py:136

commit v2 on v1

--- a/solution.py
+++ b/solution.py
@@ -14,6 +14,8 @@
 BLOCK = 256
 EPS = 1e-05
 ACROSS_LAST = (((1,), (1,)), ((), ()))
+VMEM_LIMIT = 32 * 2**20
+FREE = pl.CostEstimate(flops=0, bytes_accessed=0, transcendentals=0)
 
 
 def square_sums(y):
@@ -27,23 +29,25 @@
     )
 
 
-def first_kernel(lap_ref, norm_ref, query_ref, key_ref, value_ref, x_ref, now_ref, later_ref):
-    sums = square_sums(x_ref[...])
-    rows = [[], []]
-    for step in range(2):
-        for gain in (norm_ref, query_ref, key_ref, value_ref):
-            rows[step].append(jnp.where(lap_ref[step] == 0, gain[0:1], gain[1:2]))
-    now_ref[...] = jnp.concatenate([sums[0:1]] + rows[0] + [sums[1:4]], axis=0)
-    later_ref[...] = jnp.concatenate([sums[0:1]] + rows[1] + [sums[1:4]], axis=0)
+def first_kernel(lap_ref, norm_ref, query_ref, key_ref, value_ref, x_ref, sums_ref, now_ref, later_ref):
+    sums_ref[...] = square_sums(x_ref[...])[0:1]
+    for step, out_ref in enumerate((now_ref, later_ref)):
+        for row, gain in enumerate((norm_ref, query_ref, key_ref, value_ref)):
+            out_ref[row : row + 1] = jnp.where(lap_ref[step] == 0, gain[0:1], gain[1:2])
 
 
 def first(laps, gains, x):
-    shape = jax.ShapeDtypeStruct((8, x.shape[1]), jnp.float32)
+    width = x.shape[1]
     return pl.pallas_call(
         first_kernel,
         in_specs=[pl.BlockSpec(memory_space=pltpu.SMEM)] + [pl.BlockSpec(memory_space=pltpu.VMEM)] * 5,
-        out_shape=(shape, shape),
-        compiler_params=pltpu.CompilerParams(vmem_limit_bytes=24 * 2**20),
+        out_shape=(
+            jax.ShapeDtypeStruct((1, x.shape[0]), jnp.float32),
+            jax.ShapeDtypeStruct((4, width), jnp.float32),
+            jax.ShapeDtypeStruct((4, width), jnp.float32),
+        ),
+        compiler_params=pltpu.CompilerParams(vmem_limit_bytes=60 * 2**20),
+        cost_estimate=FREE,
     )(laps, *gains, x)
 
 
@@ -58,9 +62,9 @@
 
     def prepare(head):
         cols = slice(head * HEAD, (head + 1) * HEAD)
-        normed = x_ref[:, cols].astype(jnp.float32) * scale * gain_ref[1:2, cols]
-        query = (normed * gain_ref[2:3, cols]).astype(jnp.bfloat16)
-        keys = (normed * gain_ref[3:4, cols]).astype(jnp.bfloat16)
+        normed = x_ref[:, cols].astype(jnp.float32) * scale * gain_ref[0:1, cols]
+        query = (normed * gain_ref[1:2, cols]).astype(jnp.bfloat16)
+        keys = (normed * gain_ref[2:3, cols]).astype(jnp.bfloat16)
         return query, keys, normed.astype(jnp.bfloat16), cols
 
     def score(parts, block):
@@ -79,7 +83,7 @@
         _, _, values, cols = parts
         lo, hi = block * BLOCK, (block + 1) * BLOCK
         att = jnp.dot(probs, values[:hi], preferred_element_type=jnp.float32)
-        y_ref[lo:hi, cols] = (x_ref[lo:hi, cols].astype(jnp.float32) + gain_ref[4:5, cols] * att).astype(jnp.bfloat16)
+        y_ref[lo:hi, cols] = (x_ref[lo:hi, cols].astype(jnp.float32) + gain_ref[3:4, cols] * att).astype(jnp.bfloat16)
 
     tasks = [(head, block) for head in range(width // HEAD) for block in range(seq // BLOCK)]
     ready = {}
@@ -105,7 +109,7 @@
         rest[0][...] = square_sums(y_ref[...])
 
 
-def mixer(x, total, row, gains, first_head=0, with_sums=False):
+def mixer(x, total, row, gains, first_head=0, with_sums=False, cost=0):
     seq, width = x.shape
     out_shape = [jax.ShapeDtypeStruct(x.shape, jnp.bfloat16)]
     out_specs = [pl.BlockSpec((seq, width), lambda i: (0, 0))]
@@ -118,15 +122,13 @@
         grid=(1,),
         in_specs=[
             pl.BlockSpec(total.shape, lambda i: (0, 0)),
-            pl.BlockSpec((8, width), lambda i: (0, at)),
+            pl.BlockSpec((gains.shape[0], width), lambda i: (0, at)),
             pl.BlockSpec((seq, width), lambda i: (0, 0)),
         ],
         out_specs=out_specs,
         out_shape=out_shape,
-        compiler_params=pltpu.CompilerParams(vmem_limit_bytes=32 * 2**20),
-        cost_estimate=pl.CostEstimate(
-            flops=12 * seq * seq * width, bytes_accessed=4 * seq * width, transcendentals=seq * seq * width // HEAD
-        ),
+        compiler_params=pltpu.CompilerParams(vmem_limit_bytes=VMEM_LIMIT),
+        cost_estimate=pl.CostEstimate(flops=cost, bytes_accessed=0, transcendentals=0),
     )(total, gains, x)
     return out if with_sums else out[0]
 
@@ -147,22 +149,24 @@
     x = acts[0]
     width = x.shape[1] // 2
     laps = lax.dynamic_index_in_dim(plan, lax.axis_index("section"), 1, keepdims=False)
-    now, later = first(laps, (norm_gain[0], query_gain[0], key_gain[0], value_gain[0]), x)
-    gains_now = moved(now, 2)
-    gains_mirror = moved(now, half)
+    mirror = [moved(x[:, i * width : (i + 1) * width], half) for i in range(2)]
     behind = moved(x, 2)
-    mirror = [moved(x[:, i * width : (i + 1) * width], half) for i in range(2)]
+    sums, now, later = first(laps, (norm_gain[0], query_gain[0], key_gain[0], value_gain[0]), x)
     gains_later = moved(later, 1)
+    packet = jnp.concatenate([now, summed(sums)], axis=0)
+    packet, gains_later = lax.optimization_barrier((packet, gains_later))
+    behind_packet = moved(packet, 2)
+    mirror_packet = moved(packet, half)
 
-    totals = summed(jnp.concatenate([gains_now[0:1], gains_mirror[0:1]], axis=0))
-    once, sums = mixer(behind, totals, 0, gains_now, with_sums=True)
-    totals_later = summed(sums[0:1])
-    early, totals_later = lax.optimization_barrier((mirror[0], totals_later))
-    mixed = [mixer(early, totals, 1, gains_mirror)]
-    twice = mixer(once, totals_later, 0, gains_later)
-    late, twice = lax.optimization_barrier((mirror[1], twice))
-    mixed.append(mixer(late, totals, 1, gains_mirror, first_head=width // HEAD))
-    relayed = [moved(part, 1) for part in mixed]
+    once, sums = mixer(behind, behind_packet, 4, behind_packet, with_sums=True)
+    total = summed(sums[0:1])
+    chunk, total = lax.optimization_barrier((mirror[0], total))
+    first_part = mixer(chunk, mirror_packet, 4, mirror_packet)
+    chunk, first_part = lax.optimization_barrier((mirror[1], first_part))
+    second_part = mixer(chunk, mirror_packet, 4, mirror_packet, first_head=width // HEAD, cost=10**10)
+    relayed = [moved(first_part, 1), moved(second_part, 1)]
+    total, second_part = lax.optimization_barrier((total, second_part))
+    twice = mixer(once, total, 0, gains_later)
     stash = jnp.stack([jnp.concatenate(mirror, axis=1), jnp.concatenate(relayed, axis=1)], axis=0)
     return (twice[None], stash[None])
 

time: 135 us -> 148 us (1.096)
  the two profiles are of different devices: /device:TPU:4 before, /device:TPU:36 now
where the time goes in v2:
time: 148 us; the launch traced here: 147 us
  waiting for transfers between devices  63.9 us (43%)
  starting transfers between devices  43.2 us (29%)
  Pallas kernels  19 us (13%)
  blocking collectives  12.9 us (9%)
  local copies, waits for them, and re-layouts  4.35 us (3%)
  other arithmetic  3.27 us (2%)
    ppermute x8, waiting for transfers between devices, moved(): lax.ppermute(array, 'section', [(i, (i + by) % size) for i in range(size)])  52.1 us
    ppermute x8, starting transfers between devices, moved(): lax.ppermute(array, 'section', [(i, (i + by) % size) for i in range(size)])  22.6 us
    all_to_all x2, starting transfers between devices, summed(): lax.all_to_all(jnp.broadcast_to(part[None], (size,) + part.shape), 'z', 0...  20.6 us
    pallas_call x4, Pallas kernels, mixer(): pl.pallas_call(functools.partial(mixer_kernel, with_sums, row), grid=(1,)...  16.3 us
    psum x2, blocking collectives, summed(): return lax.psum(copies.sum(0), 'xh')  12.9 us
    all_to_all x2, waiting for transfers between devices, summed(): lax.all_to_all(jnp.broadcast_to(part[None], (size,) + part.shape), 'z', 0...  11.8 us
  transfers between devices with their start and end apart: 10, of which 6 were waited for; matrix products, arithmetic and copies ran while one was open for 4% of the time, Pallas kernels for 11%

profile of v2, /device:TPU:36, one launch (start us, length us, event | category | flops | bytes accessed | tf_op | source)
XLA Modules:
  0.0 147.4 jit_solution(18267635149830403609)
XLA Ops:
  0.6 0.0 copy-start
  0.6 3.1 %collective-permute-start.3 = (bf16[768,768]{1,0:T(8,128)(2,1)}, bf16[768,768]{1,0:T(8,128)(2,1)S(1)}, u32[]{:S(2)}, u32[]{:S(2)}) collective-permute-start(bf16[768,768]{1,0:T(8,128)(2,1)} %bitcast.12), channel_id=1, source_target_pairs={{0,32},{16,48},{32,64},{48,80},{64,96},{80,112},{96,128},{112,144}... | collective-permute-start | bytes 3538952 | tf_op jit(solution)/shard_map/ppermute | solution.py:138
  3.8 2.4 %fusion = (bf16[768,384]{1,0:T(8,128)(2,1)}, bf16[768,384]{1,0:T(8,128)(2,1)}) fusion(bf16[768,768]{1,0:T(8,128)(2,1)} %bitcast.13), kind=kLoop, calls=%fused_computation.6 | loop fusion | bytes 2359296 | tf_op jit(solution)/shard_map/slice | solution.py:152
  6.1 2.0 %collective-permute-start = (bf16[768,384]{1,0:T(8,128)(2,1)}, bf16[768,384]{1,0:T(8,128)(2,1)S(1)}, u32[]{:S(2)}, u32[]{:S(2)}) collective-permute-start(bf16[768,384]{1,0:T(8,128)(2,1)} %get-tuple-element.27), channel_id=1, source_target_pairs={{0,256},{16,272},{32,288},{48,304},{64,320},{80,336},{96,352},{112... | collective-permute-start | bytes 1769480 | tf_op jit(solution)/shard_map/ppermute | solution.py:138
  8.1 7.7 %collective-permute-start.5 = (bf16[768,384]{1,0:T(8,128)(2,1)}, bf16[768,384]{1,0:T(8,128)(2,1)S(1)}, u32[]{:S(2)}, u32[]{:S(2)}) collective-permute-start(bf16[768,384]{1,0:T(8,128)(2,1)} %get-tuple-element.26), channel_id=1, source_target_pairs={{0,256},{16,272},{32,288},{48,304},{64,320},{80,336},{96,352},{112... | collective-permute-start | bytes 1769480 | tf_op jit(solution)/shard_map/ppermute | solution.py:138
  15.9 0.0 copy-done
  15.9 0.7 dynamic-slice_reduce_fusion.lap_ref
  16.6 2.7 %shard_map.77 = (f32[1,768]{1,0:T(1,128)}, f32[4,768]{1,0:T(4,128)}, f32[4,768]{1,0:T(4,128)}) custom-call(s32[2]{0:T(128)} %dynamic-slice_reduce_fusion.lap_ref, f32[2,768]{1,0:T(2,128)} %bitcast.16, f32[2,768]{1,0:T(2,128)} %bitcast.17, f32[2,768]{1,0:T(2,128)} %bitcast.18, f32[2,768]{1,0:T(2,128)} %bitcast.19, bf16[768,768]{1,0:T(8,128)(2,1)} %bitcast.14), custom_call_target="tpu_custom_call" | custom-call | tf_op jit(solution)/shard_map/pallas_call | solution.py:41
  19.3 0.7 reduce.3
  20.0 0.6 broadcast_in_dim.23
  20.6 10.3 %all-to-all-start = ((f32[8,1,768]{2,1,0:T(1,128)}), f32[8,1,768]{2,1,0:T(1,128)S(1)}, u32[]{:S(2)}, u32[]{:S(2)}) async-start(f32[8,1,768]{2,1,0:T(1,128)} %broadcast_in_dim.23), calls=%async_computation | async-start | bytes 49152 | tf_op jit(solution)/shard_map/all_to_all | solution.py:143
  30.9 1.9 %collective-permute-start.1 = (f32[4,768]{1,0:T(4,128)}, f32[4,768]{1,0:T(4,128)S(1)}, u32[]{:S(2)}, u32[]{:S(2)}) collective-permute-start(f32[4,768]{1,0:T(4,128)} %get-tuple-element.16), channel_id=1, source_target_pairs={{0,16},{16,32},{32,48},{48,64},{64,80},{80,96},{96,112},{112,128},... | collective-permute-start | bytes 36872 | tf_op jit(solution)/shard_map/ppermute | solution.py:138
  32.9 5.9 %all-to-all-done = f32[8,1,768]{2,1,0:T(1,128)S(1)} async-done(((f32[8,1,768]{2,1,0:T(1,128)}), f32[8,1,768]{2,1,0:T(1,128)S(1)}, u32[]{:S(2)}, u32[]{:S(2)}) %all-to-all-start) | async-done | bytes 24608 | tf_op jit(solution)/shard_map/all_to_all | solution.py:143
  38.8 6.5 %psum.14 = f32[1,768]{1,0:T(1,128)S(1)} all-reduce(f32[1,768]{1,0:T(1,128)S(1)} %reduce_sum.23), channel_id=1, replica_groups=mesh['section'=32,'xh'=2,'z'=8] {'xh'}, use_global_device_ids=true, to_apply=%region_1.2 | all-reduce | flops 768 | bytes 6144 | tf_op jit(solution)/shard_map/psum | solution.py:144
  45.3 0.7 pad_maximum_fusion
  46.0 0.0 copy-start.1
  46.0 36.3 %collective-permute-done.1.gain_ref = f32[4,768]{1,0:T(4,128)S(1)} collective-permute-done((f32[4,768]{1,0:T(4,128)}, f32[4,768]{1,0:T(4,128)S(1)}, u32[]{:S(2)}, u32[]{:S(2)}) %collective-permute-start.1) | collective-permute-done | bytes 12320 | tf_op jit(solution)/shard_map/ppermute | solution.py:138
  82.2 1.9 %collective-permute-start.2 = (f32[5,768]{1,0:T(8,128)S(1)}, f32[5,768]{1,0:T(8,128)S(1)}, u32[]{:S(2)}, u32[]{:S(2)}) collective-permute-start(f32[5,768]{1,0:T(8,128)S(1)} %pad_maximum_fusion), channel_id=1, source_target_pairs={{0,32},{16,48},{32,64},{48,80},{64,96},{80,112},{96,128},{112,144}... | collective-permute-start | bytes 46088 | tf_op jit(solution)/shard_map/ppermute | solution.py:138
  84.2 5.9 %collective-permute-done.2.total_ref.gain_ref = f32[5,768]{1,0:T(8,128)S(1)} collective-permute-done((f32[5,768]{1,0:T(8,128)S(1)}, f32[5,768]{1,0:T(8,128)S(1)}, u32[]{:S(2)}, u32[]{:S(2)}) %collective-permute-start.2) | collective-permute-done | bytes 15392 | tf_op jit(solution)/shard_map/ppermute | solution.py:138
  90.1 0.0 copy-done.1
  90.1 0.0 collective-permute-done.3.x_ref
  90.1 5.5 %shard_map.78 = (bf16[768,768]{1,0:T(8,128)(2,1)S(1)}, f32[8,768]{1,0:T(8,128)S(1)}) custom-call(f32[5,768]{1,0:T(8,128)S(1)} %collective-permute-done.2.total_ref.gain_ref, f32[5,768]{1,0:T(8,128)S(1)} %collective-permute-done.2.total_ref.gain_ref, bf16[768,768]{1,0:T(8,128)(2,1)S(1)} %collective-permute-done.3.x_ref), custom_call_target="tpu_custom_call" | custom-call | tf_op jit(solution)/shard_map/pallas_call | solution.py:120
  95.6 0.6 broadcast_in_dim.25
  96.2 10.3 %all-to-all-start.1 = ((f32[8,1,768]{2,1,0:T(1,128)}), f32[8,1,768]{2,1,0:T(1,128)S(1)}, u32[]{:S(2)}, u32[]{:S(2)}) async-start(f32[8,1,768]{2,1,0:T(1,128)} %broadcast_in_dim.25), calls=%async_computation.1 | async-start | bytes 49152 | tf_op jit(solution)/shard_map/all_to_all | solution.py:143
  106.5 1.9 %collective-permute-start.4 = (f32[5,768]{1,0:T(8,128)}, f32[5,768]{1,0:T(8,128)S(1)}, u32[]{:S(2)}, u32[]{:S(2)}) collective-permute-start(f32[5,768]{1,0:T(8,128)} %copy-done.1), channel_id=1, source_target_pairs={{0,256},{16,272},{32,288},{48,304},{64,320},{80,336},{96,352},{112... | collective-permute-start | bytes 46088 | tf_op jit(solution)/shard_map/ppermute | solution.py:138
  108.4 5.9 %all-to-all-done.1 = f32[8,1,768]{2,1,0:T(1,128)S(1)} async-done(((f32[8,1,768]{2,1,0:T(1,128)}), f32[8,1,768]{2,1,0:T(1,128)S(1)}, u32[]{:S(2)}, u32[]{:S(2)}) %all-to-all-start.1) | async-done | bytes 24608 | tf_op jit(solution)/shard_map/all_to_all | solution.py:143
  114.4 6.5 %psum.15.total_ref = f32[1,768]{1,0:T(1,128)S(1)} all-reduce(f32[1,768]{1,0:T(1,128)S(1)} %reduce_sum.25), channel_id=1, replica_groups=mesh['section'=32,'xh'=2,'z'=8] {'xh'}, use_global_device_ids=true, to_apply=%region_3.4 | all-reduce | flops 768 | bytes 6144 | tf_op jit(solution)/shard_map/psum | solution.py:144
  120.8 0.0 collective-permute-done.x_ref
  120.8 0.0 collective-permute-done.4.total_ref.gain_ref
  120.8 2.6 %shard_map.79 = bf16[768,384]{1,0:T(8,128)(2,1)S(1)} custom-call(f32[5,768]{1,0:T(8,128)S(1)} %collective-permute-done.4.total_ref.gain_ref, f32[5,768]{1,0:T(8,128)S(1)} %collective-permute-done.4.total_ref.gain_ref, bf16[768,384]{1,0:T(8,128)(2,1)S(1)} %collective-permute-done.x_ref), custom_call_target="tpu_custom_call" | custom-call | tf_op jit(solution)/shard_map/pallas_call | solution.py:120
  123.5 0.0 collective-permute-done.5.x_ref
  123.5 2.6 %shard_map.80 = bf16[768,384]{1,0:T(8,128)(2,1)S(1)} custom-call(f32[5,768]{1,0:T(8,128)S(1)} %collective-permute-done.4.total_ref.gain_ref, f32[5,768]{1,0:T(8,128)S(1)} %collective-permute-done.4.total_ref.gain_ref, bf16[768,384]{1,0:T(8,128)(2,1)S(1)} %collective-permute-done.5.x_ref), custom_call_target="tpu_custom_call" | custom-call | flops 10000000000 | tf_op jit(solution)/shard_map/pallas_call | solution.py:120
  126.1 1.9 %collective-permute-start.7 = (bf16[768,384]{1,0:T(8,128)(2,1)S(1)}, bf16[768,384]{1,0:T(8,128)(2,1)S(1)}, u32[]{:S(2)}, u32[]{:S(2)}) collective-permute-start(bf16[768,384]{1,0:T(8,128)(2,1)S(1)} %shard_map.80), channel_id=1, source_target_pairs={{0,16},{16,32},{32,48},{48,64},{64,80},{80,96},{96,112},{112,128},... | collective-permute-start | bytes 1769480 | tf_op jit(solution)/shard_map/ppermute | solution.py:138
  128.0 2.1 %collective-permute-start.6 = (bf16[768,384]{1,0:T(8,128)(2,1)S(1)}, bf16[768,384]{1,0:T(8,128)(2,1)S(1)}, u32[]{:S(2)}, u32[]{:S(2)}) collective-permute-start(bf16[768,384]{1,0:T(8,128)(2,1)S(1)} %shard_map.79), channel_id=1, source_target_pairs={{0,16},{16,32},{32,48},{48,64},{64,80},{80,96},{96,112},{112,128},... | collective-permute-start | bytes 1769480 | tf_op jit(solution)/shard_map/ppermute | solution.py:138
  130.1 0.1 maximum_bitcast_fusion.1
  130.2 5.6 %shard_map.81 = bf16[768,768]{1,0:T(8,128)(2,1)} custom-call(f32[1,768]{1,0:T(1,128)S(1)} %psum.15.total_ref, f32[4,768]{1,0:T(4,128)S(1)} %collective-permute-done.1.gain_ref, bf16[768,768]{1,0:T(8,128)(2,1)S(1)} %get-tuple-element.24.x_ref), custom_call_target="tpu_custom_call" | custom-call | tf_op jit(solution)/shard_map/pallas_call | solution.py:120
  135.8 3.6 %collective-permute-done.7 = bf16[768,384]{1,0:T(8,128)(2,1)S(1)} collective-permute-done((bf16[768,384]{1,0:T(8,128)(2,1)S(1)}, bf16[768,384]{1,0:T(8,128)(2,1)S(1)}, u32[]{:S(2)}, u32[]{:S(2)}) %collective-permute-start.7) | collective-permute-done | bytes 589856 | tf_op jit(solution)/shard_map/ppermute | solution.py:138
  139.4 6.3 %collective-permute-done.6 = bf16[768,384]{1,0:T(8,128)(2,1)S(1)} collective-permute-done((bf16[768,384]{1,0:T(8,128)(2,1)S(1)}, bf16[768,384]{1,0:T(8,128)(2,1)S(1)}, u32[]{:S(2)}, u32[]{:S(2)}) %collective-permute-start.6) | collective-permute-done | bytes 589856 | tf_op jit(solution)/shard_map/ppermute | solution.py:138
  145.7 0.1 maximum_bitcast_fusion.2
  145.8 1.6 %maximum_bitcast_fusion = bf16[1,2,768,768]{3,2,1,0:T(8,128)(2,1)} fusion(bf16[1,768,768]{2,1,0:T(8,128)(2,1)S(1)} %maximum_bitcast_fusion.2, bf16[1,768,768]{2,1,0:T(8,128)(2,1)S(1)} %maximum_bitcast_fusion.1), kind=kLoop, calls=%fused_computation | loop fusion | flops 1179648 | bytes 4718592 | tf_op jit(solution)/shard_map/broadcast_in_dim | solution.py:171
  (5 shorter events, 0.1 us)
Async XLA Ops:
  0.6 15.3 %copy-start = (s32[2,32]{1,0:T(2,128)S(1)}, s32[2,32]{1,0:T(2,128)}, u32[]{:S(2)}) copy-start(s32[2,32]{1,0:T(2,128)} %param.7) | copy-start | bytes 772
  0.6 89.4 %collective-permute-start.3 = (bf16[768,768]{1,0:T(8,128)(2,1)}, bf16[768,768]{1,0:T(8,128)(2,1)S(1)}, u32[]{:S(2)}, u32[]{:S(2)}) collective-permute-start(bf16[768,768]{1,0:T(8,128)(2,1)} %bitcast.12), channel_id=1, source_target_pairs={{0,32},{16,48},{32,64},{48,80},{64,96},{80,112},{96,128},{112,144}... | collective-permute-start | bytes 3538952 | tf_op jit(solution)/shard_map/ppermute | solution.py:138
  6.1 114.7 %collective-permute-start = (bf16[768,384]{1,0:T(8,128)(2,1)}, bf16[768,384]{1,0:T(8,128)(2,1)S(1)}, u32[]{:S(2)}, u32[]{:S(2)}) collective-permute-start(bf16[768,384]{1,0:T(8,128)(2,1)} %get-tuple-element.27), channel_id=1, source_target_pairs={{0,256},{16,272},{32,288},{48,304},{64,320},{80,336},{96,352},{112... | collective-permute-start | bytes 1769480 | tf_op jit(solution)/shard_map/ppermute | solution.py:138
  8.1 115.3 %collective-permute-start.5 = (bf16[768,384]{1,0:T(8,128)(2,1)}, bf16[768,384]{1,0:T(8,128)(2,1)S(1)}, u32[]{:S(2)}, u32[]{:S(2)}) collective-permute-start(bf16[768,384]{1,0:T(8,128)(2,1)} %get-tuple-element.26), channel_id=1, source_target_pairs={{0,256},{16,272},{32,288},{48,304},{64,320},{80,336},{96,352},{112... | collective-permute-start | bytes 1769480 | tf_op jit(solution)/shard_map/ppermute | solution.py:138
  20.6 18.1 %all-to-all-start = ((f32[8,1,768]{2,1,0:T(1,128)}), f32[8,1,768]{2,1,0:T(1,128)S(1)}, u32[]{:S(2)}, u32[]{:S(2)}) async-start(f32[8,1,768]{2,1,0:T(1,128)} %broadcast_in_dim.23), calls=%async_computation | async-start | bytes 49152 | tf_op jit(solution)/shard_map/all_to_all | solution.py:143
  30.9 51.3 %collective-permute-start.1 = (f32[4,768]{1,0:T(4,128)}, f32[4,768]{1,0:T(4,128)S(1)}, u32[]{:S(2)}, u32[]{:S(2)}) collective-permute-start(f32[4,768]{1,0:T(4,128)} %get-tuple-element.16), channel_id=1, source_target_pairs={{0,16},{16,32},{32,48},{48,64},{64,80},{80,96},{96,112},{112,128},... | collective-permute-start | bytes 36872 | tf_op jit(solution)/shard_map/ppermute | solution.py:138
  46.0 44.1 %copy-start.1 = (f32[5,768]{1,0:T(8,128)}, f32[5,768]{1,0:T(8,128)S(1)}, u32[]{:S(2)}) copy-start(f32[5,768]{1,0:T(8,128)S(1)} %pad_maximum_fusion) | copy-start | bytes 46084
  82.2 7.8 %collective-permute-start.2 = (f32[5,768]{1,0:T(8,128)S(1)}, f32[5,768]{1,0:T(8,128)S(1)}, u32[]{:S(2)}, u32[]{:S(2)}) collective-permute-start(f32[5,768]{1,0:T(8,128)S(1)} %pad_maximum_fusion), channel_id=1, source_target_pairs={{0,32},{16,48},{32,64},{48,80},{64,96},{80,112},{96,128},{112,144}... | collective-permute-start | bytes 46088 | tf_op jit(solution)/shard_map/ppermute | solution.py:138
  96.2 18.1 %all-to-all-start.1 = ((f32[8,1,768]{2,1,0:T(1,128)}), f32[8,1,768]{2,1,0:T(1,128)S(1)}, u32[]{:S(2)}, u32[]{:S(2)}) async-start(f32[8,1,768]{2,1,0:T(1,128)} %broadcast_in_dim.25), calls=%async_computation.1 | async-start | bytes 49152 | tf_op jit(solution)/shard_map/all_to_all | solution.py:143
  106.5 14.3 %collective-permute-start.4 = (f32[5,768]{1,0:T(8,128)}, f32[5,768]{1,0:T(8,128)S(1)}, u32[]{:S(2)}, u32[]{:S(2)}) collective-permute-start(f32[5,768]{1,0:T(8,128)} %copy-done.1), channel_id=1, source_target_pairs={{0,256},{16,272},{32,288},{48,304},{64,320},{80,336},{96,352},{112... | collective-permute-start | bytes 46088 | tf_op jit(solution)/shard_map/ppermute | solution.py:138
  126.1 13.3 %collective-permute-start.7 = (bf16[768,384]{1,0:T(8,128)(2,1)S(1)}, bf16[768,384]{1,0:T(8,128)(2,1)S(1)}, u32[]{:S(2)}, u32[]{:S(2)}) collective-permute-start(bf16[768,384]{1,0:T(8,128)(2,1)S(1)} %shard_map.80), channel_id=1, source_target_pairs={{0,16},{16,32},{32,48},{48,64},{64,80},{80,96},{96,112},{112,128},... | collective-permute-start | bytes 1769480 | tf_op jit(solution)/shard_map/ppermute | solution.py:138
  128.0 17.7 %collective-permute-start.6 = (bf16[768,384]{1,0:T(8,128)(2,1)S(1)}, bf16[768,384]{1,0:T(8,128)(2,1)S(1)}, u32[]{:S(2)}, u32[]{:S(2)}) collective-permute-start(bf16[768,384]{1,0:T(8,128)(2,1)S(1)} %shard_map.79), channel_id=1, source_target_pairs={{0,16},{16,32},{32,48},{48,64},{64,80},{80,96},{96,112},{112,128},... | collective-permute-start | bytes 1769480 | tf_op jit(solution)/shard_map/ppermute | solution.py:138

commit v3 on v2

v3 whole, which is shorter than its diff:
```python
import functools
import math

import jax
import jax.numpy as jnp
from jax import lax
from jax.experimental import pallas as pl
from jax.experimental.pallas import tpu as pltpu
from jax.sharding import Mesh
from jax.sharding import PartitionSpec as P

D = 12288
HEAD = 128
BLOCK = 256
EPS = 1e-05
FAR = (512, 256)
TAIL = 32
ACROSS_LAST = (((1,), (1,)), ((), ()))
VMEM_LIMIT = 32 * 2**20
FREE = pl.CostEstimate(flops=0, bytes_accessed=0, transcendentals=0)


def square_sums(y):
    yf = y.astype(jnp.float32)
    squared = yf * yf
    high = squared.astype(jnp.bfloat16)
    low = (squared - high.astype(jnp.float32)).astype(jnp.bfloat16)
    ones = jnp.ones((8, y.shape[1]), jnp.bfloat16)
    sums = lax.dot_general(ones, high, ACROSS_LAST, preferred_element_type=jnp.float32) + lax.dot_general(
        ones, low, ACROSS_LAST, preferred_element_type=jnp.float32
    )
    return sums[0:1]


def thirds(value):
    high = value.astype(jnp.bfloat16).astype(jnp.float32)
    middle = (value - high).astype(jnp.bfloat16).astype(jnp.float32)
    return [high, middle, value - high - middle]


def chosen(plan_ref, step, gains):
    lap = plan_ref[step, lax.axis_index("section")]
    return jnp.concatenate([jnp.where(lap == 0, gain[0:1], gain[1:2]) for gain in gains], axis=0)


def first_kernel(plan_ref, norm_ref, query_ref, key_ref, value_ref, x_ref, now_ref, later_ref, sums_ref):
    gains = (norm_ref, query_ref, key_ref, value_ref)
    now_ref[...] = chosen(plan_ref, 0, gains)
    later_ref[...] = chosen(plan_ref, 1, gains)
    sums = square_sums(x_ref[...])
    for copy in range(sums_ref.shape[0]):
        sums_ref[copy] = sums


def first(plan, gains, x, copies):
    seq, width = x.shape
    gain = jax.ShapeDtypeStruct((4, width), jnp.float32)
    return pl.pallas_call(
        first_kernel,
        in_specs=[pl.BlockSpec(memory_space=pltpu.SMEM)] + [pl.BlockSpec(memory_space=pltpu.VMEM)] * 5,
        out_shape=(gain, gain, jax.ShapeDtypeStruct((copies, 1, seq), jnp.float32)),
        compiler_params=pltpu.CompilerParams(vmem_limit_bytes=60 * 2**20),
        cost_estimate=FREE,
    )(plan, *gains, x)


def rows_of(value, width):
    count = -(-value.shape[1] // width)
    rest = count * width - value.shape[1]
    if rest:
        value = jnp.concatenate([value, jnp.zeros((1, rest), value.dtype)], axis=1)
    return [value[:, at * width : (at + 1) * width] for at in range(count)]


def pack_kernel(total_ref, now_ref, x_ref, packet_ref, *part_refs):
    seq = x_ref.shape[0]
    packet_ref[0:4] = now_ref[...]
    packet_ref[4:5] = total_ref[...]
    col = 0
    for part_ref in part_refs:
        part = part_ref.shape[1]
        cols = slice(col, col + part)
        part_ref[:seq] = x_ref[:, cols]
        tail = thirds(now_ref[:, cols])
        for third in thirds(total_ref[...]):
            tail += rows_of(third, part)
        used = sum(rows.shape[0] for rows in tail)
        tail = jnp.concatenate(tail + [jnp.zeros((TAIL - used, part), jnp.float32)], axis=0)
        part_ref[seq:] = tail.astype(jnp.bfloat16)
        col += part


def packed(total, now, x):
    seq, width = x.shape
    parts = tuple(jax.ShapeDtypeStruct((seq + TAIL, part), jnp.bfloat16) for part in FAR)
    return pl.pallas_call(
        pack_kernel,
        out_shape=(jax.ShapeDtypeStruct((5, width), jnp.float32),) + parts,
        compiler_params=pltpu.CompilerParams(vmem_limit_bytes=VMEM_LIMIT),
        cost_estimate=FREE,
    )(total, now, x)


def unpacked(part_ref, seq):
    tail = part_ref[seq:].astype(jnp.float32)
    gains = tail[0:4] + tail[4:8] + tail[8:12]
    count = -(-seq // part_ref.shape[1])
    rows = tail[12 : 12 + count] + tail[12 + count : 12 + 2 * count] + tail[12 + 2 * count : 12 + 3 * count]
    return gains, jnp.concatenate([rows[at : at + 1] for at in range(count)], axis=1)[:, :seq]


def mixer_kernel(config, x_ref, *refs):
    plain, row, with_sums = config
    if plain:
        total_ref, gain_ref, y_ref, rest = refs[0], refs[1], refs[2], refs[3:]
        total, gain = total_ref[row : row + 1], gain_ref[...]
    else:
        y_ref, rest = refs[0], refs[1:]
        gain, total = unpacked(x_ref, y_ref.shape[0])
    seq, width = y_ref.shape
    scale = lax.rsqrt(total / D + EPS)
    scale = jnp.transpose(jnp.broadcast_to(scale, (8, seq)))[:, 0:1]
    factor = math.log2(math.e) / math.sqrt(HEAD)
    causal = lax.broadcasted_iota(jnp.int32, (BLOCK, BLOCK), 1) <= lax.broadcasted_iota(
        jnp.int32, (BLOCK, BLOCK), 0
    )

    def prepare(head):
        cols = slice(head * HEAD, (head + 1) * HEAD)
        normed = x_ref[:seq, cols].astype(jnp.float32) * scale * gain[0:1, cols]
        query = (normed * gain[1:2, cols]).astype(jnp.bfloat16)
        keys = (normed * gain[2:3, cols]).astype(jnp.bfloat16)
        return query, keys, normed.astype(jnp.bfloat16), gain[3:4, cols], cols

    def score(ready, block):
        query, keys = ready[:2]
        lo, hi = block * BLOCK, (block + 1) * BLOCK
        raw = lax.dot_general(query[lo:hi], keys[:hi], ACROSS_LAST, preferred_element_type=jnp.float32)
        last = jnp.where(causal, raw[:, lo:], -1e30)
        return jnp.concatenate([raw[:, :lo], last], axis=1) if lo else last

    def softmax(raw):
        top = jnp.max(raw, axis=1, keepdims=True)
        weights = jnp.exp2((raw - top) * factor)
        return (weights * (1.0 / jnp.sum(weights, axis=1, keepdims=True))).astype(jnp.bfloat16)

    def finish(ready, block, probs):
        values, value_gain, cols = ready[2:]
        lo, hi = block * BLOCK, (block + 1) * BLOCK
        att = jnp.dot(probs, values[:hi], preferred_element_type=jnp.float32)
        y_ref[lo:hi, cols] = (
            x_ref[lo:hi, cols].astype(jnp.float32) + value_gain * att
        ).astype(jnp.bfloat16)

    tasks = [(head, block) for head in range(width // HEAD) for block in range(seq // BLOCK)]
    prepared = {}
    scores = {}

    def issue(at):
        head, block = tasks[at]
        if head not in prepared:
            prepared[head] = prepare(head)
        scores[at] = score(prepared[head], block)

    issue(0)
    pending = None
    for at, (head, block) in enumerate(tasks):
        if at + 1 < len(tasks):
            issue(at + 1)
        probs = softmax(scores.pop(at))
        if pending is not None:
            finish(*pending)
        pending = (prepared[head], block, probs)
    finish(*pending)
    if with_sums:
        sums = square_sums(y_ref[...])
        for copy in range(rest[0].shape[0]):
            rest[0][copy] = sums


def mixer(x, seq, total=None, row=0, gains=None, copies=0):
    width = x.shape[1]
    out_shape = [jax.ShapeDtypeStruct((seq, width), jnp.bfloat16)]
    if copies:
        out_shape.append(jax.ShapeDtypeStruct((copies, 1, seq), jnp.float32))
    plain = total is not None
    operands = (x, total, gains) if plain else (x,)
    whole = lambda array: pl.BlockSpec(array.shape, lambda i: (0,) * len(array.shape))
    out = pl.pallas_call(
        functools.partial(mixer_kernel, (plain, row, copies > 0)),
        grid=(1,),
        in_specs=[whole(operand) for operand in operands],
        out_specs=[whole(shape) for shape in out_shape],
        out_shape=out_shape,
        compiler_params=pltpu.CompilerParams(vmem_limit_bytes=VMEM_LIMIT),
        cost_estimate=FREE,
    )(*operands)
    return out if copies else out[0]


def place_kernel(*refs):
    out_ref = refs[-1]
    seq = out_ref.shape[1]
    slot, col = 0, 0
    for ref in refs[:-1]:
        out_ref[slot, :, col : col + ref.shape[1]] = ref[:seq]
        col += ref.shape[1]
        if col == out_ref.shape[2]:
            slot, col = slot + 1, 0


def place(parts, shape):
    return pl.pallas_call(
        place_kernel,
        in_specs=[pl.BlockSpec(memory_space=pltpu.VMEM)] * len(parts),
        out_specs=pl.BlockSpec(memory_space=pltpu.VMEM),
        out_shape=jax.ShapeDtypeStruct(shape, jnp.bfloat16),
        compiler_params=pltpu.CompilerParams(vmem_limit_bytes=VMEM_LIMIT),
        cost_estimate=FREE,
    )(*parts)


def moved(array, target):
    size = lax.axis_size("section")
    return lax.ppermute(array, "section", [(i, target(i) % size) for i in range(size)])


def summed(copies):
    return lax.psum(lax.all_to_all(copies, "z", 0, 0, tiled=True).sum(0), "xh")


def local(acts, plan, norm_gain, query_gain, key_gain, value_gain):
    half = lax.axis_size("section") // 2
    along = lax.axis_size("z")
    x = acts[0]
    seq, width = x.shape
    gains = (norm_gain[0], query_gain[0], key_gain[0], value_gain[0])
    behind = moved(x, lambda s: s + 2)
    now, later, copies = first(plan, gains, x, along)
    gains_later = moved(later, lambda s: s + 1)
    packet, far_left, far_right = packed(summed(copies), now, x)
    packet = moved(packet, lambda s: s + 2)
    far_left, far_right, behind, packet, gains_later = lax.optimization_barrier(
        (far_left, far_right, behind, packet, gains_later)
    )
    mirror_left = moved(far_left, lambda s: s + half)
    mirror_right = moved(far_right, lambda s: s + half)

    once, copies = mixer(behind, seq, packet, 4, packet, copies=along)
    twice = mixer(once, seq, summed(copies), 0, gains_later)
    mirror_left, twice = lax.optimization_barrier((mirror_left, twice))
    left = mixer(mirror_left, seq)
    mirror_right, left = lax.optimization_barrier((mirror_right, left))
    right = mixer(mirror_right, seq)
    left = moved(left, lambda s: s + 1)
    right = moved(right, lambda s: s + 1)
    stash = place([mirror_left, mirror_right, left], (2, seq, width))
    stash = lax.dynamic_update_slice(stash, right[None], (1, 0, FAR[0]))
    return (twice[None], stash[None])


def solution(mesh):
    sections, shards = mesh.shape["section"], mesh.shape["tp"]
    fine = Mesh(mesh.devices.reshape(sections, 2, shards // 2), ("section", "xh", "z"))
    tp = ("xh", "z")
    gain = P("section", None, tp)
    return jax.shard_map(
        local,
        mesh=fine,
        in_specs=(P("section", None, tp), P(), gain, gain, gain, gain),
        out_specs=(P("section", None, tp), P("section", None, None, tp)),
        check_vma=False,
    )
```

time: 148 us -> 127 us (0.86)
  the two profiles are of different devices: /device:TPU:36 before, /device:TPU:24 now
where the time goes in v3:
time: 127 us; the launch traced here: 126 us
  blocking collectives  49.2 us (39%)
  waiting for transfers between devices  27.2 us (21%)
  starting transfers between devices  22.6 us (18%)
  Pallas kernels  21.4 us (17%)
  local copies, waits for them, and re-layouts  5.04 us (4%)
    all_to_all x2, blocking collectives, summed(): return lax.psum(lax.all_to_all(copies, 'z', 0, 0, tiled=True).sum(0), 'xh')  34.8 us
    ppermute x7, waiting for transfers between devices, moved(): lax.ppermute(array, 'section', [(i, target(i) % size) for i in range(size)])  27.2 us
    ppermute x7, starting transfers between devices, moved(): lax.ppermute(array, 'section', [(i, target(i) % size) for i in range(size)])  22.6 us
    pallas_call x4, Pallas kernels, mixer(): pl.pallas_call(functools.partial(mixer_kernel, (plain, row, copies > 0)),...  16.2 us
    psum x2, blocking collectives, summed(): return lax.psum(lax.all_to_all(copies, 'z', 0, 0, tiled=True).sum(0), 'xh')  14.4 us
    unnamed x8, local copies, waits for them, and re-layouts  4.25 us
    pallas_call x1, Pallas kernels, first(): pl.pallas_call(first_kernel, in_specs=[pl.BlockSpec(memory_space=pltpu.SM...  2.74 us
  transfers between devices with their start and end apart: 7, of which 5 were waited for; matrix products, arithmetic and copies ran while one was open for 0% of the time, Pallas kernels for 17%

profile of v3, /device:TPU:24, one launch (start us, length us, event | category | flops | bytes accessed | tf_op | source)
XLA Modules:
  0.0 126.2 jit_solution(12068378239741269499)
XLA Ops:
  0.6 3.4 %collective-permute-start = (bf16[768,768]{1,0:T(8,128)(2,1)}, bf16[768,768]{1,0:T(8,128)(2,1)S(1)}, u32[]{:S(2)}, u32[]{:S(2)}) collective-permute-start(bf16[768,768]{1,0:T(8,128)(2,1)} %bitcast.9), channel_id=1, source_target_pairs={{0,32},{16,48},{32,64},{48,80},{64,96},{80,112},{96,128},{112,144}... | collective-permute-start | bytes 3538952 | tf_op jit(solution)/shard_map/ppermute | solution.py:225
  4.0 2.7 %shard_map.77 = (f32[4,768]{1,0:T(4,128)}, f32[4,768]{1,0:T(4,128)}, f32[8,1,768]{2,1,0:T(1,128)}) custom-call(s32[2,32]{1,0:T(2,128)} %plan_ref.1, f32[2,768]{1,0:T(2,128)} %bitcast.14, f32[2,768]{1,0:T(2,128)} %bitcast.15, f32[2,768]{1,0:T(2,128)} %bitcast.16, f32[2,768]{1,0:T(2,128)} %bitcast.17, bf16[768,768]{1,0:T(8,128)(2,1)} %bitcast.10), custom_call_target="tpu_custom_call" | custom-call | tf_op jit(solution)/shard_map/pallas_call | solution.py:58
  6.8 18.1 %all_to_all.10 = f32[8,1,768]{2,1,0:T(1,128)S(1)} all-to-all(f32[8,1,768]{2,1,0:T(1,128)} %get-tuple-element.19), channel_id=1, replica_groups=mesh['section'=32,'xh'=2,'z'=8] {'z'}, dimensions={0} | all-to-all | bytes 49152 | tf_op jit(solution)/shard_map/all_to_all | solution.py:229
  25.0 7.8 %psum.14.total_ref = f32[1,768]{1,0:T(1,128)S(1)} all-reduce(f32[1,768]{1,0:T(1,128)S(1)} %reduce_sum.23), channel_id=1, replica_groups=mesh['section'=32,'xh'=2,'z'=8] {'xh'}, use_global_device_ids=true, to_apply=%region_1.0 | all-reduce | flops 768 | bytes 6144 | tf_op jit(solution)/shard_map/psum | solution.py:229
  32.7 0.0 copy-start
  32.7 1.3 %copy-done = bf16[1,768,768]{2,1,0:T(8,128)(2,1)S(1)} copy-done((bf16[1,768,768]{2,1,0:T(8,128)(2,1)S(1)}, bf16[1,768,768]{2,1,0:T(8,128)(2,1)}, u32[]{:S(2)}) %copy-start) | copy-done | bytes 1179672
  34.0 0.0 copy-start.3
  34.0 0.7 copy-done.3
  34.7 0.8 shard_map.78
  35.5 3.3 %collective-permute-start.1 = (f32[5,768]{1,0:T(8,128)S(1)}, f32[5,768]{1,0:T(8,128)S(1)}, u32[]{:S(2)}, u32[]{:S(2)}) collective-permute-start(f32[5,768]{1,0:T(8,128)S(1)} %get-tuple-element.23), channel_id=1, source_target_pairs={{0,32},{16,48},{32,64},{48,80},{64,96},{80,112},{96,128},{112,144}... | collective-permute-start | bytes 46088 | tf_op jit(solution)/shard_map/ppermute | solution.py:225
  38.9 1.9 %collective-permute-start.2 = (f32[4,768]{1,0:T(4,128)}, f32[4,768]{1,0:T(4,128)S(1)}, u32[]{:S(2)}, u32[]{:S(2)}) collective-permute-start(f32[4,768]{1,0:T(4,128)} %get-tuple-element.24), channel_id=1, source_target_pairs={{0,16},{16,32},{32,48},{48,64},{64,80},{80,96},{96,112},{112,128},... | collective-permute-start | bytes 36872 | tf_op jit(solution)/shard_map/ppermute | solution.py:225
  40.8 4.2 %collective-permute-done.2.refs_1_ = f32[4,768]{1,0:T(4,128)S(1)} collective-permute-done((f32[4,768]{1,0:T(4,128)}, f32[4,768]{1,0:T(4,128)S(1)}, u32[]{:S(2)}, u32[]{:S(2)}) %collective-permute-start.2) | collective-permute-done | bytes 12320 | tf_op jit(solution)/shard_map/ppermute | solution.py:225
  45.0 0.0 collective-permute-done.1.refs_0_.refs_1_
  45.0 0.0 collective-permute-done.x_ref
  45.0 0.0 copy-start.1
  45.0 1.0 copy-done.1
  46.0 3.6 %collective-permute-start.3 = (bf16[800,512]{1,0:T(8,128)(2,1)S(1)}, bf16[800,512]{1,0:T(8,128)(2,1)S(1)}, u32[]{:S(2)}, u32[]{:S(2)}) collective-permute-start(bf16[800,512]{1,0:T(8,128)(2,1)S(1)} %get-tuple-element.25), channel_id=1, source_target_pairs={{0,256},{16,272},{32,288},{48,304},{64,320},{80,336},{96,352},{112... | collective-permute-start | bytes 2457608 | tf_op jit(solution)/shard_map/ppermute | solution.py:225
  49.6 6.1 %collective-permute-start.4 = (bf16[800,256]{1,0:T(8,128)(2,1)}, bf16[800,256]{1,0:T(8,128)(2,1)S(1)}, u32[]{:S(2)}, u32[]{:S(2)}) collective-permute-start(bf16[800,256]{1,0:T(8,128)(2,1)} %get-tuple-element.33), channel_id=1, source_target_pairs={{0,256},{16,272},{32,288},{48,304},{64,320},{80,336},{96,352},{112... | collective-permute-start | bytes 1228808 | tf_op jit(solution)/shard_map/ppermute | solution.py:225
  55.8 0.0 copy-start.2
  55.8 1.3 copy-done.2
  57.0 5.4 %shard_map.79 = (bf16[768,768]{1,0:T(8,128)(2,1)S(1)}, f32[8,1,768]{2,1,0:T(1,128)S(1)}) custom-call(bf16[768,768]{1,0:T(8,128)(2,1)S(1)} %copy-done.2, f32[5,768]{1,0:T(8,128)S(1)} %collective-permute-done.1.refs_0_.refs_1_, f32[5,768]{1,0:T(8,128)S(1)} %collective-permute-done.1.refs_0_.refs_1_), custom_call_target="tpu_custom_call" | custom-call | tf_op jit(solution)/shard_map/pallas_call | solution.py:189
  62.5 16.7 %all_to_all.11 = f32[8,1,768]{2,1,0:T(1,128)S(1)} all-to-all(f32[8,1,768]{2,1,0:T(1,128)S(1)} %get-tuple-element.29), channel_id=1, replica_groups=mesh['section'=32,'xh'=2,'z'=8] {'z'}, dimensions={0} | all-to-all | bytes 49152 | tf_op jit(solution)/shard_map/all_to_all | solution.py:229
  79.2 6.6 %psum.15.refs_0_ = f32[1,768]{1,0:T(1,128)S(1)} all-reduce(f32[1,768]{1,0:T(1,128)S(1)} %reduce_sum.25), channel_id=1, replica_groups=mesh['section'=32,'xh'=2,'z'=8] {'xh'}, use_global_device_ids=true, to_apply=%region_3.0 | all-reduce | flops 768 | bytes 6144 | tf_op jit(solution)/shard_map/psum | solution.py:229
  85.8 5.6 %shard_map.80 = bf16[768,768]{1,0:T(8,128)(2,1)} custom-call(bf16[768,768]{1,0:T(8,128)(2,1)S(1)} %get-tuple-element.28.x_ref, f32[1,768]{1,0:T(1,128)S(1)} %psum.15.refs_0_, f32[4,768]{1,0:T(4,128)S(1)} %collective-permute-done.2.refs_1_), custom_call_target="tpu_custom_call" | custom-call | tf_op jit(solution)/shard_map/pallas_call | solution.py:189
  91.4 8.0 %collective-permute-done.3.x_ref.refs_0_ = bf16[800,512]{1,0:T(8,128)(2,1)S(1)} collective-permute-done((bf16[800,512]{1,0:T(8,128)(2,1)S(1)}, bf16[800,512]{1,0:T(8,128)(2,1)S(1)}, u32[]{:S(2)}, u32[]{:S(2)}) %collective-permute-start.3) | collective-permute-done | bytes 819232 | tf_op jit(solution)/shard_map/ppermute | solution.py:225
  99.4 3.3 %shard_map.81 = bf16[768,512]{1,0:T(8,128)(2,1)S(1)} custom-call(bf16[800,512]{1,0:T(8,128)(2,1)S(1)} %collective-permute-done.3.x_ref.refs_0_), custom_call_target="tpu_custom_call" | custom-call | tf_op jit(solution)/shard_map/pallas_call | solution.py:189
  102.7 4.3 %collective-permute-done.4.refs_1_.x_ref = bf16[800,256]{1,0:T(8,128)(2,1)S(1)} collective-permute-done((bf16[800,256]{1,0:T(8,128)(2,1)}, bf16[800,256]{1,0:T(8,128)(2,1)S(1)}, u32[]{:S(2)}, u32[]{:S(2)}) %collective-permute-start.4) | collective-permute-done | bytes 409632 | tf_op jit(solution)/shard_map/ppermute | solution.py:225
  107.0 1.9 %collective-permute-start.5 = (bf16[768,512]{1,0:T(8,128)(2,1)S(1)}, bf16[768,512]{1,0:T(8,128)(2,1)S(1)}, u32[]{:S(2)}, u32[]{:S(2)}) collective-permute-start(bf16[768,512]{1,0:T(8,128)(2,1)S(1)} %shard_map.81), channel_id=1, source_target_pairs={{0,16},{16,32},{32,48},{48,64},{64,80},{80,96},{96,112},{112,128},... | collective-permute-start | bytes 2359304 | tf_op jit(solution)/shard_map/ppermute | solution.py:225
  108.9 1.9 %shard_map.83 = bf16[768,256]{1,0:T(8,128)(2,1)S(1)} custom-call(bf16[800,256]{1,0:T(8,128)(2,1)S(1)} %collective-permute-done.4.refs_1_.x_ref), custom_call_target="tpu_custom_call" | custom-call | tf_op jit(solution)/shard_map/pallas_call | solution.py:189
  110.9 2.4 %collective-permute-start.6 = (bf16[768,256]{1,0:T(8,128)(2,1)S(1)}, bf16[768,256]{1,0:T(8,128)(2,1)S(1)}, u32[]{:S(2)}, u32[]{:S(2)}) collective-permute-start(bf16[768,256]{1,0:T(8,128)(2,1)S(1)} %shard_map.83), channel_id=1, source_target_pairs={{0,16},{16,32},{32,48},{48,64},{64,80},{80,96},{96,112},{112,128},... | collective-permute-start | bytes 1179656 | tf_op jit(solution)/shard_map/ppermute | solution.py:225
  113.3 8.0 %collective-permute-done.5.refs_2_ = bf16[768,512]{1,0:T(8,128)(2,1)S(1)} collective-permute-done((bf16[768,512]{1,0:T(8,128)(2,1)S(1)}, bf16[768,512]{1,0:T(8,128)(2,1)S(1)}, u32[]{:S(2)}, u32[]{:S(2)}) %collective-permute-start.5) | collective-permute-done | bytes 786464 | tf_op jit(solution)/shard_map/ppermute | solution.py:225
  121.2 1.5 %shard_map.82 = bf16[2,768,768]{2,1,0:T(8,128)(2,1)} custom-call(bf16[800,512]{1,0:T(8,128)(2,1)S(1)} %collective-permute-done.3.x_ref.refs_0_, bf16[800,256]{1,0:T(8,128)(2,1)S(1)} %collective-permute-done.4.refs_1_.x_ref, bf16[768,512]{1,0:T(8,128)(2,1)S(1)} %collective-permute-done.5.refs_2_), custom_call_target="tpu_custom_call" | custom-call | tf_op jit(solution)/shard_map/pallas_call | solution.py:213
  122.8 2.7 %collective-permute-done.6 = bf16[768,256]{1,0:T(8,128)(2,1)S(1)} collective-permute-done((bf16[768,256]{1,0:T(8,128)(2,1)S(1)}, bf16[768,256]{1,0:T(8,128)(2,1)S(1)}, u32[]{:S(2)}, u32[]{:S(2)}) %collective-permute-start.6) | collective-permute-done | bytes 393248 | tf_op jit(solution)/shard_map/ppermute | solution.py:225
  125.4 0.8 bitcast_dynamic-update-slice_fusion
  (4 shorter events, 0.1 us)
Async XLA Ops:
  0.6 44.4 %collective-permute-start = (bf16[768,768]{1,0:T(8,128)(2,1)}, bf16[768,768]{1,0:T(8,128)(2,1)S(1)}, u32[]{:S(2)}, u32[]{:S(2)}) collective-permute-start(bf16[768,768]{1,0:T(8,128)(2,1)} %bitcast.9), channel_id=1, source_target_pairs={{0,32},{16,48},{32,64},{48,80},{64,96},{80,112},{96,128},{112,144}... | collective-permute-start | bytes 3538952 | tf_op jit(solution)/shard_map/ppermute | solution.py:225
  32.7 1.3 %copy-start = (bf16[1,768,768]{2,1,0:T(8,128)(2,1)S(1)}, bf16[1,768,768]{2,1,0:T(8,128)(2,1)}, u32[]{:S(2)}) copy-start(bf16[1,768,768]{2,1,0:T(8,128)(2,1)} %param.6) | copy-start | bytes 3538948
  34.0 0.7 copy-start.3
  35.5 9.5 %collective-permute-start.1 = (f32[5,768]{1,0:T(8,128)S(1)}, f32[5,768]{1,0:T(8,128)S(1)}, u32[]{:S(2)}, u32[]{:S(2)}) collective-permute-start(f32[5,768]{1,0:T(8,128)S(1)} %get-tuple-element.23), channel_id=1, source_target_pairs={{0,32},{16,48},{32,64},{48,80},{64,96},{80,112},{96,128},{112,144}... | collective-permute-start | bytes 46088 | tf_op jit(solution)/shard_map/ppermute | solution.py:225
  38.9 6.1 %collective-permute-start.2 = (f32[4,768]{1,0:T(4,128)}, f32[4,768]{1,0:T(4,128)S(1)}, u32[]{:S(2)}, u32[]{:S(2)}) collective-permute-start(f32[4,768]{1,0:T(4,128)} %get-tuple-element.24), channel_id=1, source_target_pairs={{0,16},{16,32},{32,48},{48,64},{64,80},{80,96},{96,112},{112,128},... | collective-permute-start | bytes 36872 | tf_op jit(solution)/shard_map/ppermute | solution.py:225
  45.0 1.0 copy-start.1
  46.0 53.4 %collective-permute-start.3 = (bf16[800,512]{1,0:T(8,128)(2,1)S(1)}, bf16[800,512]{1,0:T(8,128)(2,1)S(1)}, u32[]{:S(2)}, u32[]{:S(2)}) collective-permute-start(bf16[800,512]{1,0:T(8,128)(2,1)S(1)} %get-tuple-element.25), channel_id=1, source_target_pairs={{0,256},{16,272},{32,288},{48,304},{64,320},{80,336},{96,352},{112... | collective-permute-start | bytes 2457608 | tf_op jit(solution)/shard_map/ppermute | solution.py:225
  49.6 57.4 %collective-permute-start.4 = (bf16[800,256]{1,0:T(8,128)(2,1)}, bf16[800,256]{1,0:T(8,128)(2,1)S(1)}, u32[]{:S(2)}, u32[]{:S(2)}) collective-permute-start(bf16[800,256]{1,0:T(8,128)(2,1)} %get-tuple-element.33), channel_id=1, source_target_pairs={{0,256},{16,272},{32,288},{48,304},{64,320},{80,336},{96,352},{112... | collective-permute-start | bytes 1228808 | tf_op jit(solution)/shard_map/ppermute | solution.py:225
  55.8 1.3 %copy-start.2 = (bf16[768,768]{1,0:T(8,128)(2,1)S(1)}, bf16[768,768]{1,0:T(8,128)(2,1)}, u32[]{:S(2)}) copy-start(bf16[768,768]{1,0:T(8,128)(2,1)} %copy-done.1) | copy-start | bytes 3538948
  107.0 14.2 %collective-permute-start.5 = (bf16[768,512]{1,0:T(8,128)(2,1)S(1)}, bf16[768,512]{1,0:T(8,128)(2,1)S(1)}, u32[]{:S(2)}, u32[]{:S(2)}) collective-permute-start(bf16[768,512]{1,0:T(8,128)(2,1)S(1)} %shard_map.81), channel_id=1, source_target_pairs={{0,16},{16,32},{32,48},{48,64},{64,80},{80,96},{96,112},{112,128},... | collective-permute-start | bytes 2359304 | tf_op jit(solution)/shard_map/ppermute | solution.py:225
  110.9 14.5 %collective-permute-start.6 = (bf16[768,256]{1,0:T(8,128)(2,1)S(1)}, bf16[768,256]{1,0:T(8,128)(2,1)S(1)}, u32[]{:S(2)}, u32[]{:S(2)}) collective-permute-start(bf16[768,256]{1,0:T(8,128)(2,1)S(1)} %shard_map.83), channel_id=1, source_target_pairs={{0,16},{16,32},{32,48},{48,64},{64,80},{80,96},{96,112},{112,128},... | collective-permute-start | bytes 1179656 | tf_op jit(solution)/shard_map/ppermute | solution.py:225

commit v4 on v3

--- a/solution.py
+++ b/solution.py
@@ -43,22 +43,33 @@
     return jnp.concatenate([jnp.where(lap == 0, gain[0:1], gain[1:2]) for gain in gains], axis=0)
 
 
-def first_kernel(plan_ref, norm_ref, query_ref, key_ref, value_ref, x_ref, now_ref, later_ref, sums_ref):
+def first_kernel(plan_ref, norm_ref, query_ref, key_ref, value_ref, x_ref, now_ref, later_ref, sums_ref, *part_refs):
+    seq = x_ref.shape[0]
     gains = (norm_ref, query_ref, key_ref, value_ref)
-    now_ref[...] = chosen(plan_ref, 0, gains)
-    later_ref[...] = chosen(plan_ref, 1, gains)
+    now = chosen(plan_ref, 0, gains)
+    now_ref[...] = now
     sums = square_sums(x_ref[...])
     for copy in range(sums_ref.shape[0]):
         sums_ref[copy] = sums
+    later_ref[...] = chosen(plan_ref, 1, gains)
+    col = 0
+    for part_ref in part_refs:
+        part = part_ref.shape[1]
+        cols = slice(col, col + part)
+        part_ref[:seq] = x_ref[:, cols]
+        tail = thirds(now[:, cols]) + [jnp.zeros((TAIL - 12, part), jnp.float32)]
+        part_ref[seq:] = jnp.concatenate(tail, axis=0).astype(jnp.bfloat16)
+        col += part
 
 
 def first(plan, gains, x, copies):
     seq, width = x.shape
     gain = jax.ShapeDtypeStruct((4, width), jnp.float32)
+    parts = tuple(jax.ShapeDtypeStruct((seq + TAIL, part), jnp.bfloat16) for part in FAR)
     return pl.pallas_call(
         first_kernel,
         in_specs=[pl.BlockSpec(memory_space=pltpu.SMEM)] + [pl.BlockSpec(memory_space=pltpu.VMEM)] * 5,
-        out_shape=(gain, gain, jax.ShapeDtypeStruct((copies, 1, seq), jnp.float32)),
+        out_shape=(gain, gain, jax.ShapeDtypeStruct((copies, 1, seq), jnp.float32)) + parts,
         compiler_params=pltpu.CompilerParams(vmem_limit_bytes=60 * 2**20),
         cost_estimate=FREE,
     )(plan, *gains, x)
@@ -72,33 +83,34 @@
     return [value[:, at * width : (at + 1) * width] for at in range(count)]
 
 
-def pack_kernel(total_ref, now_ref, x_ref, packet_ref, *part_refs):
-    seq = x_ref.shape[0]
+def pack_kernel(total_ref, now_ref, *refs):
+    count = len(refs) // 2
+    packet_ref = refs[count]
     packet_ref[0:4] = now_ref[...]
     packet_ref[4:5] = total_ref[...]
-    col = 0
-    for part_ref in part_refs:
-        part = part_ref.shape[1]
-        cols = slice(col, col + part)
-        part_ref[:seq] = x_ref[:, cols]
-        tail = thirds(now_ref[:, cols])
-        for third in thirds(total_ref[...]):
-            tail += rows_of(third, part)
-        used = sum(rows.shape[0] for rows in tail)
-        tail = jnp.concatenate(tail + [jnp.zeros((TAIL - used, part), jnp.float32)], axis=0)
-        part_ref[seq:] = tail.astype(jnp.bfloat16)
-        col += part
-
-
-def packed(total, now, x):
-    seq, width = x.shape
-    parts = tuple(jax.ShapeDtypeStruct((seq + TAIL, part), jnp.bfloat16) for part in FAR)
+    for tail_ref, out_ref in zip(refs[:count], refs[count + 1 :]):
+        part = out_ref.shape[1]
+        rows = [piece for third in thirds(total_ref[...]) for piece in rows_of(third, part)]
+        used = 12 + len(rows)
+        tail = [tail_ref[0:12].astype(jnp.float32)] + rows + [jnp.zeros((TAIL - used, part), jnp.float32)]
+        out_ref[...] = jnp.concatenate(tail, axis=0).astype(jnp.bfloat16)
+
+
+def packed(total, now, parts):
+    specs = [pl.BlockSpec((TAIL, part.shape[1]), lambda i, at=part.shape[0] // TAIL - 1: (at, 0)) for part in parts]
+    whole = lambda shape: pl.BlockSpec(shape, lambda i: (0, 0))
+    packet = (5, now.shape[1])
     return pl.pallas_call(
         pack_kernel,
-        out_shape=(jax.ShapeDtypeStruct((5, width), jnp.float32),) + parts,
-        compiler_params=pltpu.CompilerParams(vmem_limit_bytes=VMEM_LIMIT),
-        cost_estimate=FREE,
-    )(total, now, x)
+        grid=(1,),
+        in_specs=[whole(total.shape), whole(now.shape)] + specs,
+        out_specs=[whole(packet)] + specs,
+        out_shape=[jax.ShapeDtypeStruct(packet, jnp.float32)]
+        + [jax.ShapeDtypeStruct(part.shape, part.dtype) for part in parts],
+        input_output_aliases={2 + at: 1 + at for at in range(len(parts))},
+        compiler_params=pltpu.CompilerParams(vmem_limit_bytes=60 * 2**20),
+        cost_estimate=FREE,
+    )(total, now, *parts)
 
 
 def unpacked(part_ref, seq):
@@ -236,21 +248,20 @@
     seq, width = x.shape
     gains = (norm_gain[0], query_gain[0], key_gain[0], value_gain[0])
     behind = moved(x, lambda s: s + 2)
-    now, later, copies = first(plan, gains, x, along)
+    now, later, copies, *parts = first(plan, gains, x, along)
     gains_later = moved(later, lambda s: s + 1)
-    packet, far_left, far_right = packed(summed(copies), now, x)
+    total, gains_later = lax.optimization_barrier((summed(copies), gains_later))
+    packet, far_left, far_right = packed(total, now, parts)
     packet = moved(packet, lambda s: s + 2)
-    far_left, far_right, behind, packet, gains_later = lax.optimization_barrier(
-        (far_left, far_right, behind, packet, gains_later)
-    )
+    far_left, far_right, behind, packet = lax.optimization_barrier((far_left, far_right, behind, packet))
     mirror_left = moved(far_left, lambda s: s + half)
+
+    once, copies = mixer(behind, seq, packet, 4, packet, copies=along)
     mirror_right = moved(far_right, lambda s: s + half)
-
-    once, copies = mixer(behind, seq, packet, 4, packet, copies=along)
     twice = mixer(once, seq, summed(copies), 0, gains_later)
     mirror_left, twice = lax.optimization_barrier((mirror_left, twice))
     left = mixer(mirror_left, seq)
-    mirror_right, left = lax.optimization_barrier((mirror_right, left))
+    mirror_right, _ = lax.optimization_barrier((mirror_right, left))
     right = mixer(mirror_right, seq)
     left = moved(left, lambda s: s + 1)
     right = moved(right, lambda s: s + 1)

time: 127 us -> 121 us (0.953)
  the two profiles are of different devices: /device:TPU:24 before, /device:TPU:448 now
where the time goes in v4:
time: 121 us
  waiting for transfers between devices  40.7 us (34%)
  starting transfers between devices  29.8 us (25%)
  blocking collectives  23.3 us (19%)
  Pallas kernels  23.1 us (19%)
  local copies, waits for them, and re-layouts  3.06 us (3%)
    ppermute x7, waiting for transfers between devices, moved(): lax.ppermute(array, 'section', [(i, target(i) % size) for i in range(size)])  34.4 us
    psum x2, blocking collectives, summed(): return lax.psum(lax.all_to_all(copies, 'z', 0, 0, tiled=True).sum(0), 'xh')  23.3 us
    ppermute x7, starting transfers between devices, moved(): lax.ppermute(array, 'section', [(i, target(i) % size) for i in range(size)])  20.8 us
    pallas_call x4, Pallas kernels, mixer(): pl.pallas_call(functools.partial(mixer_kernel, (plain, row, copies > 0)),...  17 us
    all_to_all x2, starting transfers between devices, summed(): return lax.psum(lax.all_to_all(copies, 'z', 0, 0, tiled=True).sum(0), 'xh')  9.02 us
    all_to_all x2, waiting for transfers between devices, summed(): return lax.psum(lax.all_to_all(copies, 'z', 0, 0, tiled=True).sum(0), 'xh')  6.34 us
    pallas_call x1, Pallas kernels, first(): pl.pallas_call(first_kernel, in_specs=[pl.BlockSpec(memory_space=pltpu.SM...  3.1 us
  transfers between devices with their start and end apart: 9, of which 7 were waited for; matrix products, arithmetic and copies ran while one was open for 0% of the time, Pallas kernels for 19%

profile of v4, /device:TPU:448, one launch (start us, length us, event | category | flops | bytes accessed | tf_op | source)
XLA Modules:
  0.0 120.7 jit_solution(4935270986328440631)
XLA Ops:
  0.6 3.4 %collective-permute-start.1 = (bf16[768,768]{1,0:T(8,128)(2,1)}, bf16[768,768]{1,0:T(8,128)(2,1)S(1)}, u32[]{:S(2)}, u32[]{:S(2)}) collective-permute-start(bf16[768,768]{1,0:T(8,128)(2,1)} %bitcast.11), channel_id=1, source_target_pairs={{0,32},{16,48},{32,64},{48,80},{64,96},{80,112},{96,128},{112,144}... | collective-permute-start | bytes 3538952 | tf_op jit(solution)/shard_map/ppermute | solution.py:237
  4.0 3.1 %shard_map.77 = (f32[4,768]{1,0:T(4,128)}, f32[4,768]{1,0:T(4,128)}, f32[8,1,768]{2,1,0:T(1,128)}, bf16[800,512]{1,0:T(8,128)(2,1)}, bf16[800,256]{1,0:T(8,128)(2,1)}) custom-call(s32[2,32]{1,0:T(2,128)} %plan_ref.1, f32[2,768]{1,0:T(2,128)} %bitcast.13, f32[2,768]{1,0:T(2,128)} %bitcast.14, f32[2,768]{1,0:T(2,128)} %bitcast.15, f32[2,768]{1,0:T(2,128)} %bitcast.16, ...), custom_call_target="tpu_custom_call" | custom-call | tf_op jit(solution)/shard_map/pallas_call | solution.py:69
  7.1 4.5 %all-to-all-start = ((f32[8,1,768]{2,1,0:T(1,128)}), f32[8,1,768]{2,1,0:T(1,128)S(1)}, u32[]{:S(2)}, u32[]{:S(2)}) async-start(f32[8,1,768]{2,1,0:T(1,128)} %get-tuple-element.21), calls=%async_computation | async-start | bytes 49152 | tf_op jit(solution)/shard_map/all_to_all | solution.py:241
  11.7 1.9 %collective-permute-start = (f32[4,768]{1,0:T(4,128)}, f32[4,768]{1,0:T(4,128)S(1)}, u32[]{:S(2)}, u32[]{:S(2)}) collective-permute-start(f32[4,768]{1,0:T(4,128)} %get-tuple-element.22), channel_id=1, source_target_pairs={{0,16},{16,32},{32,48},{48,64},{64,80},{80,96},{96,112},{112,128},... | collective-permute-start | bytes 36872 | tf_op jit(solution)/shard_map/ppermute | solution.py:237
  13.6 3.2 %all-to-all-done = f32[8,1,768]{2,1,0:T(1,128)S(1)} async-done(((f32[8,1,768]{2,1,0:T(1,128)}), f32[8,1,768]{2,1,0:T(1,128)S(1)}, u32[]{:S(2)}, u32[]{:S(2)}) %all-to-all-start) | async-done | bytes 24608 | tf_op jit(solution)/shard_map/all_to_all | solution.py:241
  16.8 16.6 %psum.14.total_ref = f32[1,768]{1,0:T(1,128)} all-reduce(f32[1,768]{1,0:T(1,128)S(1)} %reduce_sum.23), channel_id=1, replica_groups=mesh['section'=32,'xh'=2,'z'=8] {'xh'}, use_global_device_ids=true, to_apply=%region_1.0 | all-reduce | flops 768 | bytes 6144 | tf_op jit(solution)/shard_map/psum | solution.py:241
  33.5 0.0 collective-permute-done.refs_1_
  33.5 1.4 %shard_map.78 = (f32[5,768]{1,0:T(8,128)}, bf16[800,512]{1,0:T(8,128)(2,1)}, bf16[800,256]{1,0:T(8,128)(2,1)}) custom-call(f32[1,768]{1,0:T(1,128)} %psum.14.total_ref, f32[4,768]{1,0:T(4,128)} %get-tuple-element.24.now_ref, bf16[800,512]{1,0:T(8,128)(2,1)} %get-tuple-element.25.refs_0_, ...), custom_call_target="tpu_custom_call", output_to_operand_aliasing={{1}: (2, {}), {2}: (3, {})} | custom-call | tf_op jit(solution)/shard_map/pallas_call | solution.py:103
  34.9 1.9 %collective-permute-start.2 = (f32[5,768]{1,0:T(8,128)}, f32[5,768]{1,0:T(8,128)S(1)}, u32[]{:S(2)}, u32[]{:S(2)}) collective-permute-start(f32[5,768]{1,0:T(8,128)} %get-tuple-element.29), channel_id=1, source_target_pairs={{0,32},{16,48},{32,64},{48,80},{64,96},{80,112},{96,128},{112,144}... | collective-permute-start | bytes 46088 | tf_op jit(solution)/shard_map/ppermute | solution.py:237
  36.8 6.1 %collective-permute-done.2.refs_0_.refs_1_ = f32[5,768]{1,0:T(8,128)S(1)} collective-permute-done((f32[5,768]{1,0:T(8,128)}, f32[5,768]{1,0:T(8,128)S(1)}, u32[]{:S(2)}, u32[]{:S(2)}) %collective-permute-start.2) | collective-permute-done | bytes 15392 | tf_op jit(solution)/shard_map/ppermute | solution.py:237
  42.9 0.0 collective-permute-done.1.x_ref
  42.9 0.0 copy-start
  42.9 1.0 copy-done
  43.9 7.7 %collective-permute-start.3 = (bf16[800,512]{1,0:T(8,128)(2,1)}, bf16[800,512]{1,0:T(8,128)(2,1)S(1)}, u32[]{:S(2)}, u32[]{:S(2)}) collective-permute-start(bf16[800,512]{1,0:T(8,128)(2,1)} %get-tuple-element.30), channel_id=1, source_target_pairs={{0,256},{16,272},{32,288},{48,304},{64,320},{80,336},{96,352},{112... | collective-permute-start | bytes 2457608 | tf_op jit(solution)/shard_map/ppermute | solution.py:237
  51.7 0.0 copy-start.1
  51.7 1.3 %copy-done.1 = bf16[768,768]{1,0:T(8,128)(2,1)S(1)} copy-done((bf16[768,768]{1,0:T(8,128)(2,1)S(1)}, bf16[768,768]{1,0:T(8,128)(2,1)}, u32[]{:S(2)}) %copy-start.1) | copy-done | bytes 1179672
  52.9 6.1 %shard_map.79 = (bf16[768,768]{1,0:T(8,128)(2,1)S(1)}, f32[8,1,768]{2,1,0:T(1,128)}) custom-call(bf16[768,768]{1,0:T(8,128)(2,1)S(1)} %copy-done.1, f32[5,768]{1,0:T(8,128)S(1)} %collective-permute-done.2.refs_0_.refs_1_, f32[5,768]{1,0:T(8,128)S(1)} %collective-permute-done.2.refs_0_.refs_1_), custom_call_target="tpu_custom_call" | custom-call | tf_op jit(solution)/shard_map/pallas_call | solution.py:201
  59.0 4.5 %all-to-all-start.1 = ((f32[8,1,768]{2,1,0:T(1,128)}), f32[8,1,768]{2,1,0:T(1,128)S(1)}, u32[]{:S(2)}, u32[]{:S(2)}) async-start(f32[8,1,768]{2,1,0:T(1,128)} %get-tuple-element.34), calls=%async_computation.1 | async-start | bytes 49152 | tf_op jit(solution)/shard_map/all_to_all | solution.py:241
  63.5 2.0 %collective-permute-start.4 = (bf16[800,256]{1,0:T(8,128)(2,1)}, bf16[800,256]{1,0:T(8,128)(2,1)S(1)}, u32[]{:S(2)}, u32[]{:S(2)}) collective-permute-start(bf16[800,256]{1,0:T(8,128)(2,1)} %get-tuple-element.38), channel_id=1, source_target_pairs={{0,256},{16,272},{32,288},{48,304},{64,320},{80,336},{96,352},{112... | collective-permute-start | bytes 1228808 | tf_op jit(solution)/shard_map/ppermute | solution.py:237
  65.5 3.1 %all-to-all-done.1 = f32[8,1,768]{2,1,0:T(1,128)S(1)} async-done(((f32[8,1,768]{2,1,0:T(1,128)}), f32[8,1,768]{2,1,0:T(1,128)S(1)}, u32[]{:S(2)}, u32[]{:S(2)}) %all-to-all-start.1) | async-done | bytes 24608 | tf_op jit(solution)/shard_map/all_to_all | solution.py:241
  68.7 6.6 %psum.15.refs_0_ = f32[1,768]{1,0:T(1,128)S(1)} all-reduce(f32[1,768]{1,0:T(1,128)S(1)} %reduce_sum.25), channel_id=1, replica_groups=mesh['section'=32,'xh'=2,'z'=8] {'xh'}, use_global_device_ids=true, to_apply=%region_3.0 | all-reduce | flops 768 | bytes 6144 | tf_op jit(solution)/shard_map/psum | solution.py:241
  75.3 5.7 %shard_map.80 = bf16[768,768]{1,0:T(8,128)(2,1)} custom-call(bf16[768,768]{1,0:T(8,128)(2,1)S(1)} %get-tuple-element.33.x_ref, f32[1,768]{1,0:T(1,128)S(1)} %psum.15.refs_0_, f32[4,768]{1,0:T(4,128)S(1)} %collective-permute-done.refs_1_), custom_call_target="tpu_custom_call" | custom-call | tf_op jit(solution)/shard_map/pallas_call | solution.py:201
  81.0 16.0 %collective-permute-done.3.x_ref.refs_0_ = bf16[800,512]{1,0:T(8,128)(2,1)S(1)} collective-permute-done((bf16[800,512]{1,0:T(8,128)(2,1)}, bf16[800,512]{1,0:T(8,128)(2,1)S(1)}, u32[]{:S(2)}, u32[]{:S(2)}) %collective-permute-start.3) | collective-permute-done | bytes 819232 | tf_op jit(solution)/shard_map/ppermute | solution.py:237
  97.0 3.3 %shard_map.81 = bf16[768,512]{1,0:T(8,128)(2,1)S(1)} custom-call(bf16[800,512]{1,0:T(8,128)(2,1)S(1)} %collective-permute-done.3.x_ref.refs_0_), custom_call_target="tpu_custom_call" | custom-call | tf_op jit(solution)/shard_map/pallas_call | solution.py:201
  100.3 1.9 %collective-permute-start.5 = (bf16[768,512]{1,0:T(8,128)(2,1)S(1)}, bf16[768,512]{1,0:T(8,128)(2,1)S(1)}, u32[]{:S(2)}, u32[]{:S(2)}) collective-permute-start(bf16[768,512]{1,0:T(8,128)(2,1)S(1)} %shard_map.81), channel_id=1, source_target_pairs={{0,16},{16,32},{32,48},{48,64},{64,80},{80,96},{96,112},{112,128},... | collective-permute-start | bytes 2359304 | tf_op jit(solution)/shard_map/ppermute | solution.py:237
  102.2 1.3 %collective-permute-done.4.refs_1_.x_ref = bf16[800,256]{1,0:T(8,128)(2,1)S(1)} collective-permute-done((bf16[800,256]{1,0:T(8,128)(2,1)}, bf16[800,256]{1,0:T(8,128)(2,1)S(1)}, u32[]{:S(2)}, u32[]{:S(2)}) %collective-permute-start.4) | collective-permute-done | bytes 409632 | tf_op jit(solution)/shard_map/ppermute | solution.py:237
  103.6 2.0 %shard_map.83 = bf16[768,256]{1,0:T(8,128)(2,1)S(1)} custom-call(bf16[800,256]{1,0:T(8,128)(2,1)S(1)} %collective-permute-done.4.refs_1_.x_ref), custom_call_target="tpu_custom_call" | custom-call | tf_op jit(solution)/shard_map/pallas_call | solution.py:201
  105.6 1.9 %collective-permute-start.6 = (bf16[768,256]{1,0:T(8,128)(2,1)S(1)}, bf16[768,256]{1,0:T(8,128)(2,1)S(1)}, u32[]{:S(2)}, u32[]{:S(2)}) collective-permute-start(bf16[768,256]{1,0:T(8,128)(2,1)S(1)} %shard_map.83), channel_id=1, source_target_pairs={{0,16},{16,32},{32,48},{48,64},{64,80},{80,96},{96,112},{112,128},... | collective-permute-start | bytes 1179656 | tf_op jit(solution)/shard_map/ppermute | solution.py:237
  107.5 8.2 %collective-permute-done.5.refs_2_ = bf16[768,512]{1,0:T(8,128)(2,1)S(1)} collective-permute-done((bf16[768,512]{1,0:T(8,128)(2,1)S(1)}, bf16[768,512]{1,0:T(8,128)(2,1)S(1)}, u32[]{:S(2)}, u32[]{:S(2)}) %collective-permute-start.5) | collective-permute-done | bytes 786464 | tf_op jit(solution)/shard_map/ppermute | solution.py:237
  115.7 1.5 %shard_map.82 = bf16[2,768,768]{2,1,0:T(8,128)(2,1)} custom-call(bf16[800,512]{1,0:T(8,128)(2,1)S(1)} %collective-permute-done.3.x_ref.refs_0_, bf16[800,256]{1,0:T(8,128)(2,1)S(1)} %collective-permute-done.4.refs_1_.x_ref, bf16[768,512]{1,0:T(8,128)(2,1)S(1)} %collective-permute-done.5.refs_2_), custom_call_target="tpu_custom_call" | custom-call | tf_op jit(solution)/shard_map/pallas_call | solution.py:225
  117.3 2.7 %collective-permute-done.6 = bf16[768,256]{1,0:T(8,128)(2,1)S(1)} collective-permute-done((bf16[768,256]{1,0:T(8,128)(2,1)S(1)}, bf16[768,256]{1,0:T(8,128)(2,1)S(1)}, u32[]{:S(2)}, u32[]{:S(2)}) %collective-permute-start.6) | collective-permute-done | bytes 393248 | tf_op jit(solution)/shard_map/ppermute | solution.py:237
  119.9 0.8 bitcast_dynamic-update-slice_fusion
  (4 shorter events, 0.1 us)
Async XLA Ops:
  0.6 42.3 %collective-permute-start.1 = (bf16[768,768]{1,0:T(8,128)(2,1)}, bf16[768,768]{1,0:T(8,128)(2,1)S(1)}, u32[]{:S(2)}, u32[]{:S(2)}) collective-permute-start(bf16[768,768]{1,0:T(8,128)(2,1)} %bitcast.11), channel_id=1, source_target_pairs={{0,32},{16,48},{32,64},{48,80},{64,96},{80,112},{96,128},{112,144}... | collective-permute-start | bytes 3538952 | tf_op jit(solution)/shard_map/ppermute | solution.py:237
  7.1 9.6 %all-to-all-start = ((f32[8,1,768]{2,1,0:T(1,128)}), f32[8,1,768]{2,1,0:T(1,128)S(1)}, u32[]{:S(2)}, u32[]{:S(2)}) async-start(f32[8,1,768]{2,1,0:T(1,128)} %get-tuple-element.21), calls=%async_computation | async-start | bytes 49152 | tf_op jit(solution)/shard_map/all_to_all | solution.py:241
  11.7 21.8 %collective-permute-start = (f32[4,768]{1,0:T(4,128)}, f32[4,768]{1,0:T(4,128)S(1)}, u32[]{:S(2)}, u32[]{:S(2)}) collective-permute-start(f32[4,768]{1,0:T(4,128)} %get-tuple-element.22), channel_id=1, source_target_pairs={{0,16},{16,32},{32,48},{48,64},{64,80},{80,96},{96,112},{112,128},... | collective-permute-start | bytes 36872 | tf_op jit(solution)/shard_map/ppermute | solution.py:237
  34.9 8.0 %collective-permute-start.2 = (f32[5,768]{1,0:T(8,128)}, f32[5,768]{1,0:T(8,128)S(1)}, u32[]{:S(2)}, u32[]{:S(2)}) collective-permute-start(f32[5,768]{1,0:T(8,128)} %get-tuple-element.29), channel_id=1, source_target_pairs={{0,32},{16,48},{32,64},{48,80},{64,96},{80,112},{96,128},{112,144}... | collective-permute-start | bytes 46088 | tf_op jit(solution)/shard_map/ppermute | solution.py:237
  42.9 1.0 copy-start
  43.9 53.0 %collective-permute-start.3 = (bf16[800,512]{1,0:T(8,128)(2,1)}, bf16[800,512]{1,0:T(8,128)(2,1)S(1)}, u32[]{:S(2)}, u32[]{:S(2)}) collective-permute-start(bf16[800,512]{1,0:T(8,128)(2,1)} %get-tuple-element.30), channel_id=1, source_target_pairs={{0,256},{16,272},{32,288},{48,304},{64,320},{80,336},{96,352},{112... | collective-permute-start | bytes 2457608 | tf_op jit(solution)/shard_map/ppermute | solution.py:237
  51.7 1.3 %copy-start.1 = (bf16[768,768]{1,0:T(8,128)(2,1)S(1)}, bf16[768,768]{1,0:T(8,128)(2,1)}, u32[]{:S(2)}) copy-start(bf16[768,768]{1,0:T(8,128)(2,1)} %copy-done) | copy-start | bytes 3538948
  59.0 9.6 %all-to-all-start.1 = ((f32[8,1,768]{2,1,0:T(1,128)}), f32[8,1,768]{2,1,0:T(1,128)S(1)}, u32[]{:S(2)}, u32[]{:S(2)}) async-start(f32[8,1,768]{2,1,0:T(1,128)} %get-tuple-element.34), calls=%async_computation.1 | async-start | bytes 49152 | tf_op jit(solution)/shard_map/all_to_all | solution.py:241
  63.5 40.1 %collective-permute-start.4 = (bf16[800,256]{1,0:T(8,128)(2,1)}, bf16[800,256]{1,0:T(8,128)(2,1)S(1)}, u32[]{:S(2)}, u32[]{:S(2)}) collective-permute-start(bf16[800,256]{1,0:T(8,128)(2,1)} %get-tuple-element.38), channel_id=1, source_target_pairs={{0,256},{16,272},{32,288},{48,304},{64,320},{80,336},{96,352},{112... | collective-permute-start | bytes 1228808 | tf_op jit(solution)/shard_map/ppermute | solution.py:237
  100.3 15.4 %collective-permute-start.5 = (bf16[768,512]{1,0:T(8,128)(2,1)S(1)}, bf16[768,512]{1,0:T(8,128)(2,1)S(1)}, u32[]{:S(2)}, u32[]{:S(2)}) collective-permute-start(bf16[768,512]{1,0:T(8,128)(2,1)S(1)} %shard_map.81), channel_id=1, source_target_pairs={{0,16},{16,32},{32,48},{48,64},{64,80},{80,96},{96,112},{112,128},... | collective-permute-start | bytes 2359304 | tf_op jit(solution)/shard_map/ppermute | solution.py:237
  105.6 14.4 %collective-permute-start.6 = (bf16[768,256]{1,0:T(8,128)(2,1)S(1)}, bf16[768,256]{1,0:T(8,128)(2,1)S(1)}, u32[]{:S(2)}, u32[]{:S(2)}) collective-permute-start(bf16[768,256]{1,0:T(8,128)(2,1)S(1)} %shard_map.83), channel_id=1, source_target_pairs={{0,16},{16,32},{32,48},{48,64},{64,80},{80,96},{96,112},{112,128},... | collective-permute-start | bytes 1179656 | tf_op jit(solution)/shard_map/ppermute | solution.py:237

commit v5 on v4

--- a/solution.py
+++ b/solution.py
@@ -13,7 +13,7 @@
 HEAD = 128
 BLOCK = 256
 EPS = 1e-05
-FAR = (512, 256)
+FAR = (256, 256, 256)
 TAIL = 32
 ACROSS_LAST = (((1,), (1,)), ((), ()))
 VMEM_LIMIT = 32 * 2**20
@@ -251,22 +251,22 @@
     now, later, copies, *parts = first(plan, gains, x, along)
     gains_later = moved(later, lambda s: s + 1)
     total, gains_later = lax.optimization_barrier((summed(copies), gains_later))
-    packet, far_left, far_right = packed(total, now, parts)
+    packet, *far = packed(total, now, parts)
     packet = moved(packet, lambda s: s + 2)
-    far_left, far_right, behind, packet = lax.optimization_barrier((far_left, far_right, behind, packet))
-    mirror_left = moved(far_left, lambda s: s + half)
+    *far, behind, packet = lax.optimization_barrier((*far, behind, packet))
+    mirror = [moved(part, lambda s: s + half) for part in far]
 
     once, copies = mixer(behind, seq, packet, 4, packet, copies=along)
-    mirror_right = moved(far_right, lambda s: s + half)
-    twice = mixer(once, seq, summed(copies), 0, gains_later)
-    mirror_left, twice = lax.optimization_barrier((mirror_left, twice))
-    left = mixer(mirror_left, seq)
-    mirror_right, _ = lax.optimization_barrier((mirror_right, left))
-    right = mixer(mirror_right, seq)
-    left = moved(left, lambda s: s + 1)
-    right = moved(right, lambda s: s + 1)
-    stash = place([mirror_left, mirror_right, left], (2, seq, width))
-    stash = lax.dynamic_update_slice(stash, right[None], (1, 0, FAR[0]))
+    total = summed(copies)
+    before, relayed = total, []
+    for part in mirror:
+        part, _ = lax.optimization_barrier((part, before))
+        before = mixer(part, seq)
+        relayed.append(moved(before, lambda s: s + 1))
+    total, _ = lax.optimization_barrier((total, before))
+    twice = mixer(once, seq, total, 0, gains_later)
+    stash = place(mirror + relayed[:-1], (2, seq, width))
+    stash = lax.dynamic_update_slice(stash, relayed[-1][None], (1, 0, width - FAR[-1]))
     return (twice[None], stash[None])
 
 

time: 121 us -> 118 us (0.975)
  waiting for transfers between devices: 40.7 us -> 23.1 us
  blocking collectives: 23.3 us -> 32.5 us
  starting transfers between devices: 29.8 us -> 35.1 us
    ppermute x7 -> x9, waiting for transfers between devices: 34.4 us -> 19.9 us  [moved(): lax.ppermute(array, 'section', [(i, target(i) % size) for i in range(size)])]
    ppermute x7 -> x9, starting transfers between devices: 20.8 us -> 30.6 us  [moved(): lax.ppermute(array, 'section', [(i, target(i) % size) for i in range(size)])]
    all_to_all x0 -> x1, blocking collectives: none -> 9.47 us  [summed(): return lax.psum(lax.all_to_all(copies, 'z', 0, 0, tiled=True).sum(0), 'xh')]
    all_to_all x2 -> x1, starting transfers between devices: 9.02 us -> 4.51 us  [summed(): return lax.psum(lax.all_to_all(copies, 'z', 0, 0, tiled=True).sum(0), 'xh')]
    all_to_all x2 -> x1, waiting for transfers between devices: 6.34 us -> 3.22 us  [summed(): return lax.psum(lax.all_to_all(copies, 'z', 0, 0, tiled=True).sum(0), 'xh')]
    pallas_call x4 -> x5, Pallas kernels: 17 us -> 17 us  [mixer(): pl.pallas_call(functools.partial(mixer_kernel, (plain, row, copies > 0)),...]
  transfers between devices with their start and end apart: 9 -> 10, of which waited for: 7 -> 5; matrix products, arithmetic and copies ran while one was open for 0% -> 0% of each run, Pallas kernels for 19% -> 20%
where the time goes in v5:
time: 118 us
  starting transfers between devices  35.1 us (30%)
  blocking collectives  32.5 us (28%)
  Pallas kernels  23.1 us (20%)
  waiting for transfers between devices  23.1 us (20%)
  local copies, waits for them, and re-layouts  3.06 us (3%)
    ppermute x9, starting transfers between devices, moved(): lax.ppermute(array, 'section', [(i, target(i) % size) for i in range(size)])  30.6 us
    psum x2, blocking collectives, summed(): return lax.psum(lax.all_to_all(copies, 'z', 0, 0, tiled=True).sum(0), 'xh')  23.1 us
    ppermute x9, waiting for transfers between devices, moved(): lax.ppermute(array, 'section', [(i, target(i) % size) for i in range(size)])  19.9 us
    pallas_call x5, Pallas kernels, mixer(): pl.pallas_call(functools.partial(mixer_kernel, (plain, row, copies > 0)),...  17 us
    all_to_all x1, blocking collectives, summed(): return lax.psum(lax.all_to_all(copies, 'z', 0, 0, tiled=True).sum(0), 'xh')  9.47 us
    all_to_all x1, starting transfers between devices, summed(): return lax.psum(lax.all_to_all(copies, 'z', 0, 0, tiled=True).sum(0), 'xh')  4.51 us
    all_to_all x1, waiting for transfers between devices, summed(): return lax.psum(lax.all_to_all(copies, 'z', 0, 0, tiled=True).sum(0), 'xh')  3.22 us
    pallas_call x1, Pallas kernels, first(): pl.pallas_call(first_kernel, in_specs=[pl.BlockSpec(memory_space=pltpu.SM...  3.1 us
  transfers between devices with their start and end apart: 10, of which 5 were waited for; matrix products, arithmetic and copies ran while one was open for 0% of the time, Pallas kernels for 20%

profile of v5, /device:TPU:448, one launch (start us, length us, event | category | flops | bytes accessed | tf_op | source)
XLA Modules:
  0.0 117.7 jit_solution(5992826022923648198)
XLA Ops:
  0.6 3.4 %collective-permute-start.1 = (bf16[768,768]{1,0:T(8,128)(2,1)}, bf16[768,768]{1,0:T(8,128)(2,1)S(1)}, u32[]{:S(2)}, u32[]{:S(2)}) collective-permute-start(bf16[768,768]{1,0:T(8,128)(2,1)} %bitcast.11), channel_id=1, source_target_pairs={{0,32},{16,48},{32,64},{48,80},{64,96},{80,112},{96,128},{112,144}... | collective-permute-start | bytes 3538952 | tf_op jit(solution)/shard_map/ppermute | solution.py:237
  4.0 3.1 %shard_map.77 = (f32[4,768]{1,0:T(4,128)}, f32[4,768]{1,0:T(4,128)}, f32[8,1,768]{2,1,0:T(1,128)}, bf16[800,256]{1,0:T(8,128)(2,1)}, bf16[800,256]{1,0:T(8,128)(2,1)}, /*index=5*/bf16[800,256]{1,0:T(8,128)(2,1)}) custom-call(s32[2,32]{1,0:T(2,128)} %plan_ref.1, f32[2,768]{1,0:T(2,128)} %bitcast.13, f32[2,768]{1,0:T(2,128)} %bitcast.14, f32[2,768]{1,0:T(2,128)} %bitcast.15, ...), custom_call_target="tpu_custom_call" | custom-call | tf_op jit(solution)/shard_map/pallas_call | solution.py:69
  7.1 4.5 %all-to-all-start = ((f32[8,1,768]{2,1,0:T(1,128)}), f32[8,1,768]{2,1,0:T(1,128)S(1)}, u32[]{:S(2)}, u32[]{:S(2)}) async-start(f32[8,1,768]{2,1,0:T(1,128)} %get-tuple-element.25), calls=%async_computation | async-start | bytes 49152 | tf_op jit(solution)/shard_map/all_to_all | solution.py:241
  11.7 1.9 %collective-permute-start = (f32[4,768]{1,0:T(4,128)}, f32[4,768]{1,0:T(4,128)S(1)}, u32[]{:S(2)}, u32[]{:S(2)}) collective-permute-start(f32[4,768]{1,0:T(4,128)} %get-tuple-element.26), channel_id=1, source_target_pairs={{0,16},{16,32},{32,48},{48,64},{64,80},{80,96},{96,112},{112,128},... | collective-permute-start | bytes 36872 | tf_op jit(solution)/shard_map/ppermute | solution.py:237
  13.6 3.2 %all-to-all-done = f32[8,1,768]{2,1,0:T(1,128)S(1)} async-done(((f32[8,1,768]{2,1,0:T(1,128)}), f32[8,1,768]{2,1,0:T(1,128)S(1)}, u32[]{:S(2)}, u32[]{:S(2)}) %all-to-all-start) | async-done | bytes 24608 | tf_op jit(solution)/shard_map/all_to_all | solution.py:241
  16.8 16.6 %psum.14.total_ref = f32[1,768]{1,0:T(1,128)} all-reduce(f32[1,768]{1,0:T(1,128)S(1)} %reduce_sum.23), channel_id=1, replica_groups=mesh['section'=32,'xh'=2,'z'=8] {'xh'}, use_global_device_ids=true, to_apply=%region_1.0 | all-reduce | flops 768 | bytes 6144 | tf_op jit(solution)/shard_map/psum | solution.py:241
  33.4 0.0 collective-permute-done.refs_1_
  33.4 1.4 %shard_map.78 = (f32[5,768]{1,0:T(8,128)}, bf16[800,256]{1,0:T(8,128)(2,1)}, bf16[800,256]{1,0:T(8,128)(2,1)}, bf16[800,256]{1,0:T(8,128)(2,1)}) custom-call(f32[1,768]{1,0:T(1,128)} %psum.14.total_ref, f32[4,768]{1,0:T(4,128)} %get-tuple-element.28.now_ref, ...), custom_call_target="tpu_custom_call", output_to_operand_aliasing={{1}: (2, {}), {2}: (3, {}), {3}: (4, {})} | custom-call | tf_op jit(solution)/shard_map/pallas_call | solution.py:103
  34.9 1.9 %collective-permute-start.2 = (f32[5,768]{1,0:T(8,128)}, f32[5,768]{1,0:T(8,128)S(1)}, u32[]{:S(2)}, u32[]{:S(2)}) collective-permute-start(f32[5,768]{1,0:T(8,128)} %get-tuple-element.35), channel_id=1, source_target_pairs={{0,32},{16,48},{32,64},{48,80},{64,96},{80,112},{96,128},{112,144}... | collective-permute-start | bytes 46088 | tf_op jit(solution)/shard_map/ppermute | solution.py:237
  36.8 6.1 %collective-permute-done.2.refs_0_.refs_1_ = f32[5,768]{1,0:T(8,128)S(1)} collective-permute-done((f32[5,768]{1,0:T(8,128)}, f32[5,768]{1,0:T(8,128)S(1)}, u32[]{:S(2)}, u32[]{:S(2)}) %collective-permute-start.2) | collective-permute-done | bytes 15392 | tf_op jit(solution)/shard_map/ppermute | solution.py:237
  42.9 0.0 collective-permute-done.1.x_ref
  42.9 0.0 copy-start
  42.9 1.0 copy-done
  43.9 7.7 %collective-permute-start.5 = (bf16[800,256]{1,0:T(8,128)(2,1)}, bf16[800,256]{1,0:T(8,128)(2,1)S(1)}, u32[]{:S(2)}, u32[]{:S(2)}) collective-permute-start(bf16[800,256]{1,0:T(8,128)(2,1)} %get-tuple-element.42), channel_id=1, source_target_pairs={{0,256},{16,272},{32,288},{48,304},{64,320},{80,336},{96,352},{112... | collective-permute-start | bytes 1228808 | tf_op jit(solution)/shard_map/ppermute | solution.py:237
  51.6 2.0 %collective-permute-start.4 = (bf16[800,256]{1,0:T(8,128)(2,1)}, bf16[800,256]{1,0:T(8,128)(2,1)S(1)}, u32[]{:S(2)}, u32[]{:S(2)}) collective-permute-start(bf16[800,256]{1,0:T(8,128)(2,1)} %get-tuple-element.41), channel_id=1, source_target_pairs={{0,256},{16,272},{32,288},{48,304},{64,320},{80,336},{96,352},{112... | collective-permute-start | bytes 1228808 | tf_op jit(solution)/shard_map/ppermute | solution.py:237
  53.7 7.7 %collective-permute-start.3 = (bf16[800,256]{1,0:T(8,128)(2,1)}, bf16[800,256]{1,0:T(8,128)(2,1)S(1)}, u32[]{:S(2)}, u32[]{:S(2)}) collective-permute-start(bf16[800,256]{1,0:T(8,128)(2,1)} %get-tuple-element.40), channel_id=1, source_target_pairs={{0,256},{16,272},{32,288},{48,304},{64,320},{80,336},{96,352},{112... | collective-permute-start | bytes 1228808 | tf_op jit(solution)/shard_map/ppermute | solution.py:237
  61.4 0.0 copy-start.1
  61.4 1.3 %copy-done.1 = bf16[768,768]{1,0:T(8,128)(2,1)S(1)} copy-done((bf16[768,768]{1,0:T(8,128)(2,1)S(1)}, bf16[768,768]{1,0:T(8,128)(2,1)}, u32[]{:S(2)}) %copy-start.1) | copy-done | bytes 1179672
  62.7 5.5 %shard_map.79 = (bf16[768,768]{1,0:T(8,128)(2,1)S(1)}, f32[8,1,768]{2,1,0:T(1,128)S(1)}) custom-call(bf16[768,768]{1,0:T(8,128)(2,1)S(1)} %copy-done.1, f32[5,768]{1,0:T(8,128)S(1)} %collective-permute-done.2.refs_0_.refs_1_, f32[5,768]{1,0:T(8,128)S(1)} %collective-permute-done.2.refs_0_.refs_1_), custom_call_target="tpu_custom_call" | custom-call | tf_op jit(solution)/shard_map/pallas_call | solution.py:201
  68.2 9.5 %all_to_all.10 = f32[8,1,768]{2,1,0:T(1,128)S(1)} all-to-all(f32[8,1,768]{2,1,0:T(1,128)S(1)} %get-tuple-element.39), channel_id=1, replica_groups=mesh['section'=32,'xh'=2,'z'=8] {'z'}, dimensions={0} | all-to-all | bytes 49152 | tf_op jit(solution)/shard_map/all_to_all | solution.py:241
  77.7 6.4 %psum.15.refs_0_ = f32[1,768]{1,0:T(1,128)S(1)} all-reduce(f32[1,768]{1,0:T(1,128)S(1)} %reduce_sum.25), channel_id=1, replica_groups=mesh['section'=32,'xh'=2,'z'=8] {'xh'}, use_global_device_ids=true, to_apply=%region_3.0 | all-reduce | flops 768 | bytes 6144 | tf_op jit(solution)/shard_map/psum | solution.py:241
  84.2 0.0 collective-permute-done.5.x_ref.refs_0_
  84.2 2.0 %shard_map.80 = bf16[768,256]{1,0:T(8,128)(2,1)S(1)} custom-call(bf16[800,256]{1,0:T(8,128)(2,1)S(1)} %collective-permute-done.5.x_ref.refs_0_), custom_call_target="tpu_custom_call" | custom-call | tf_op jit(solution)/shard_map/pallas_call | solution.py:201
  86.1 1.9 %collective-permute-start.6 = (bf16[768,256]{1,0:T(8,128)(2,1)S(1)}, bf16[768,256]{1,0:T(8,128)(2,1)S(1)}, u32[]{:S(2)}, u32[]{:S(2)}) collective-permute-start(bf16[768,256]{1,0:T(8,128)(2,1)S(1)} %shard_map.80), channel_id=1, source_target_pairs={{0,16},{16,32},{32,48},{48,64},{64,80},{80,96},{96,112},{112,128},... | collective-permute-start | bytes 1179656 | tf_op jit(solution)/shard_map/ppermute | solution.py:237
  88.1 8.9 %collective-permute-done.4.x_ref.refs_1_ = bf16[800,256]{1,0:T(8,128)(2,1)S(1)} collective-permute-done((bf16[800,256]{1,0:T(8,128)(2,1)}, bf16[800,256]{1,0:T(8,128)(2,1)S(1)}, u32[]{:S(2)}, u32[]{:S(2)}) %collective-permute-start.4) | collective-permute-done | bytes 409632 | tf_op jit(solution)/shard_map/ppermute | solution.py:237
  97.0 2.0 %shard_map.81 = bf16[768,256]{1,0:T(8,128)(2,1)S(1)} custom-call(bf16[800,256]{1,0:T(8,128)(2,1)S(1)} %collective-permute-done.4.x_ref.refs_1_), custom_call_target="tpu_custom_call" | custom-call | tf_op jit(solution)/shard_map/pallas_call | solution.py:201
  98.9 1.9 %collective-permute-start.7 = (bf16[768,256]{1,0:T(8,128)(2,1)S(1)}, bf16[768,256]{1,0:T(8,128)(2,1)S(1)}, u32[]{:S(2)}, u32[]{:S(2)}) collective-permute-start(bf16[768,256]{1,0:T(8,128)(2,1)S(1)} %shard_map.81), channel_id=1, source_target_pairs={{0,16},{16,32},{32,48},{48,64},{64,80},{80,96},{96,112},{112,128},... | collective-permute-start | bytes 1179656 | tf_op jit(solution)/shard_map/ppermute | solution.py:237
  100.8 2.7 %collective-permute-done.3.x_ref.refs_2_ = bf16[800,256]{1,0:T(8,128)(2,1)S(1)} collective-permute-done((bf16[800,256]{1,0:T(8,128)(2,1)}, bf16[800,256]{1,0:T(8,128)(2,1)S(1)}, u32[]{:S(2)}, u32[]{:S(2)}) %collective-permute-start.3) | collective-permute-done | bytes 409632 | tf_op jit(solution)/shard_map/ppermute | solution.py:237
  103.6 2.0 %shard_map.82 = bf16[768,256]{1,0:T(8,128)(2,1)S(1)} custom-call(bf16[800,256]{1,0:T(8,128)(2,1)S(1)} %collective-permute-done.3.x_ref.refs_2_), custom_call_target="tpu_custom_call" | custom-call | tf_op jit(solution)/shard_map/pallas_call | solution.py:201
  105.5 2.1 %collective-permute-start.8 = (bf16[768,256]{1,0:T(8,128)(2,1)S(1)}, bf16[768,256]{1,0:T(8,128)(2,1)S(1)}, u32[]{:S(2)}, u32[]{:S(2)}) collective-permute-start(bf16[768,256]{1,0:T(8,128)(2,1)S(1)} %shard_map.82), channel_id=1, source_target_pairs={{0,16},{16,32},{32,48},{48,64},{64,80},{80,96},{96,112},{112,128},... | collective-permute-start | bytes 1179656 | tf_op jit(solution)/shard_map/ppermute | solution.py:237
  107.6 5.6 %shard_map.83 = bf16[768,768]{1,0:T(8,128)(2,1)} custom-call(bf16[768,768]{1,0:T(8,128)(2,1)S(1)} %get-tuple-element.38.x_ref, f32[1,768]{1,0:T(1,128)S(1)} %psum.15.refs_0_, f32[4,768]{1,0:T(4,128)S(1)} %collective-permute-done.refs_1_), custom_call_target="tpu_custom_call" | custom-call | tf_op jit(solution)/shard_map/pallas_call | solution.py:201
  113.3 0.0 collective-permute-done.7.refs_4_
  113.3 0.0 collective-permute-done.6.refs_3_
  113.3 1.5 %shard_map.84 = bf16[2,768,768]{2,1,0:T(8,128)(2,1)} custom-call(bf16[800,256]{1,0:T(8,128)(2,1)S(1)} %collective-permute-done.5.x_ref.refs_0_, bf16[800,256]{1,0:T(8,128)(2,1)S(1)} %collective-permute-done.4.x_ref.refs_1_, bf16[800,256]{1,0:T(8,128)(2,1)S(1)} %collective-permute-done.3.x_ref.refs_2_, bf16[768,256]{1,0:T(8,128)(2,1)S(1)} %collective-permute-done.6.refs_3_, ...), custom_call_target="tpu_custom_call" | custom-call | tf_op jit(solution)/shard_map/pallas_call | solution.py:225
  114.8 2.1 %collective-permute-done.8 = bf16[768,256]{1,0:T(8,128)(2,1)S(1)} collective-permute-done((bf16[768,256]{1,0:T(8,128)(2,1)S(1)}, bf16[768,256]{1,0:T(8,128)(2,1)S(1)}, u32[]{:S(2)}, u32[]{:S(2)}) %collective-permute-start.8) | collective-permute-done | bytes 393248 | tf_op jit(solution)/shard_map/ppermute | solution.py:237
  116.9 0.8 bitcast_dynamic-update-slice_fusion
  (4 shorter events, 0.1 us)
Async XLA Ops:
  0.6 42.3 %collective-permute-start.1 = (bf16[768,768]{1,0:T(8,128)(2,1)}, bf16[768,768]{1,0:T(8,128)(2,1)S(1)}, u32[]{:S(2)}, u32[]{:S(2)}) collective-permute-start(bf16[768,768]{1,0:T(8,128)(2,1)} %bitcast.11), channel_id=1, source_target_pairs={{0,32},{16,48},{32,64},{48,80},{64,96},{80,112},{96,128},{112,144}... | collective-permute-start | bytes 3538952 | tf_op jit(solution)/shard_map/ppermute | solution.py:237
  7.1 9.6 %all-to-all-start = ((f32[8,1,768]{2,1,0:T(1,128)}), f32[8,1,768]{2,1,0:T(1,128)S(1)}, u32[]{:S(2)}, u32[]{:S(2)}) async-start(f32[8,1,768]{2,1,0:T(1,128)} %get-tuple-element.25), calls=%async_computation | async-start | bytes 49152 | tf_op jit(solution)/shard_map/all_to_all | solution.py:241
  11.7 21.8 %collective-permute-start = (f32[4,768]{1,0:T(4,128)}, f32[4,768]{1,0:T(4,128)S(1)}, u32[]{:S(2)}, u32[]{:S(2)}) collective-permute-start(f32[4,768]{1,0:T(4,128)} %get-tuple-element.26), channel_id=1, source_target_pairs={{0,16},{16,32},{32,48},{48,64},{64,80},{80,96},{96,112},{112,128},... | collective-permute-start | bytes 36872 | tf_op jit(solution)/shard_map/ppermute | solution.py:237
  34.9 8.0 %collective-permute-start.2 = (f32[5,768]{1,0:T(8,128)}, f32[5,768]{1,0:T(8,128)S(1)}, u32[]{:S(2)}, u32[]{:S(2)}) collective-permute-start(f32[5,768]{1,0:T(8,128)} %get-tuple-element.35), channel_id=1, source_target_pairs={{0,32},{16,48},{32,64},{48,80},{64,96},{80,112},{96,128},{112,144}... | collective-permute-start | bytes 46088 | tf_op jit(solution)/shard_map/ppermute | solution.py:237
  42.9 1.0 copy-start
  43.9 40.3 %collective-permute-start.5 = (bf16[800,256]{1,0:T(8,128)(2,1)}, bf16[800,256]{1,0:T(8,128)(2,1)S(1)}, u32[]{:S(2)}, u32[]{:S(2)}) collective-permute-start(bf16[800,256]{1,0:T(8,128)(2,1)} %get-tuple-element.42), channel_id=1, source_target_pairs={{0,256},{16,272},{32,288},{48,304},{64,320},{80,336},{96,352},{112... | collective-permute-start | bytes 1228808 | tf_op jit(solution)/shard_map/ppermute | solution.py:237
  51.6 45.3 %collective-permute-start.4 = (bf16[800,256]{1,0:T(8,128)(2,1)}, bf16[800,256]{1,0:T(8,128)(2,1)S(1)}, u32[]{:S(2)}, u32[]{:S(2)}) collective-permute-start(bf16[800,256]{1,0:T(8,128)(2,1)} %get-tuple-element.41), channel_id=1, source_target_pairs={{0,256},{16,272},{32,288},{48,304},{64,320},{80,336},{96,352},{112... | collective-permute-start | bytes 1228808 | tf_op jit(solution)/shard_map/ppermute | solution.py:237
  53.7 49.9 %collective-permute-start.3 = (bf16[800,256]{1,0:T(8,128)(2,1)}, bf16[800,256]{1,0:T(8,128)(2,1)S(1)}, u32[]{:S(2)}, u32[]{:S(2)}) collective-permute-start(bf16[800,256]{1,0:T(8,128)(2,1)} %get-tuple-element.40), channel_id=1, source_target_pairs={{0,256},{16,272},{32,288},{48,304},{64,320},{80,336},{96,352},{112... | collective-permute-start | bytes 1228808 | tf_op jit(solution)/shard_map/ppermute | solution.py:237
  61.4 1.3 %copy-start.1 = (bf16[768,768]{1,0:T(8,128)(2,1)S(1)}, bf16[768,768]{1,0:T(8,128)(2,1)}, u32[]{:S(2)}) copy-start(bf16[768,768]{1,0:T(8,128)(2,1)} %copy-done) | copy-start | bytes 3538948
  86.1 27.1 %collective-permute-start.6 = (bf16[768,256]{1,0:T(8,128)(2,1)S(1)}, bf16[768,256]{1,0:T(8,128)(2,1)S(1)}, u32[]{:S(2)}, u32[]{:S(2)}) collective-permute-start(bf16[768,256]{1,0:T(8,128)(2,1)S(1)} %shard_map.80), channel_id=1, source_target_pairs={{0,16},{16,32},{32,48},{48,64},{64,80},{80,96},{96,112},{112,128},... | collective-permute-start | bytes 1179656 | tf_op jit(solution)/shard_map/ppermute | solution.py:237
  98.9 14.3 %collective-permute-start.7 = (bf16[768,256]{1,0:T(8,128)(2,1)S(1)}, bf16[768,256]{1,0:T(8,128)(2,1)S(1)}, u32[]{:S(2)}, u32[]{:S(2)}) collective-permute-start(bf16[768,256]{1,0:T(8,128)(2,1)S(1)} %shard_map.81), channel_id=1, source_target_pairs={{0,16},{16,32},{32,48},{48,64},{64,80},{80,96},{96,112},{112,128},... | collective-permute-start | bytes 1179656 | tf_op jit(solution)/shard_map/ppermute | solution.py:237
  105.5 11.4 %collective-permute-start.8 = (bf16[768,256]{1,0:T(8,128)(2,1)S(1)}, bf16[768,256]{1,0:T(8,128)(2,1)S(1)}, u32[]{:S(2)}, u32[]{:S(2)}) collective-permute-start(bf16[768,256]{1,0:T(8,128)(2,1)S(1)} %shard_map.82), channel_id=1, source_target_pairs={{0,16},{16,32},{32,48},{48,64},{64,80},{80,96},{96,112},{112,128},... | collective-permute-start | bytes 1179656 | tf_op jit(solution)/shard_map/ppermute | solution.py:237

commit v6 on v5

--- a/solution.py
+++ b/solution.py
@@ -16,7 +16,7 @@
 FAR = (256, 256, 256)
 TAIL = 32
 ACROSS_LAST = (((1,), (1,)), ((), ()))
-VMEM_LIMIT = 32 * 2**20
+VMEM_LIMIT = 52 * 2**20
 FREE = pl.CostEstimate(flops=0, bytes_accessed=0, transcendentals=0)
 
 

time: 118 us -> 118 us (level)
  local copies, waits for them, and re-layouts: 3.06 us -> 1.8 us
    unnamed x4 -> x2, local copies, waits for them, and re-layouts: 2.28 us -> 1.01 us
  transfers between devices with their start and end apart: 10 -> 10, of which waited for: 5 -> 5; matrix products, arithmetic and copies ran while one was open for 0% -> 0% of each run, Pallas kernels for 20% -> 21%
where the time goes in v6:
time: 118 us
  starting transfers between devices  35.1 us (30%)
  blocking collectives  32.5 us (28%)
  Pallas kernels  24.2 us (21%)
  waiting for transfers between devices  23 us (19%)
  local copies, waits for them, and re-layouts  1.8 us (2%)
    ppermute x9, starting transfers between devices, moved(): lax.ppermute(array, 'section', [(i, target(i) % size) for i in range(size)])  30.6 us
    psum x2, blocking collectives, summed(): return lax.psum(lax.all_to_all(copies, 'z', 0, 0, tiled=True).sum(0), 'xh')  23.1 us
    ppermute x9, waiting for transfers between devices, moved(): lax.ppermute(array, 'section', [(i, target(i) % size) for i in range(size)])  19.8 us
    pallas_call x5, Pallas kernels, mixer(): pl.pallas_call(functools.partial(mixer_kernel, (plain, row, copies > 0)),...  18.2 us
    all_to_all x1, blocking collectives, summed(): return lax.psum(lax.all_to_all(copies, 'z', 0, 0, tiled=True).sum(0), 'xh')  9.47 us
    all_to_all x1, starting transfers between devices, summed(): return lax.psum(lax.all_to_all(copies, 'z', 0, 0, tiled=True).sum(0), 'xh')  4.51 us
    all_to_all x1, waiting for transfers between devices, summed(): return lax.psum(lax.all_to_all(copies, 'z', 0, 0, tiled=True).sum(0), 'xh')  3.22 us
    pallas_call x1, Pallas kernels, first(): pl.pallas_call(first_kernel, in_specs=[pl.BlockSpec(memory_space=pltpu.SM...  3.1 us
  transfers between devices with their start and end apart: 10, of which 5 were waited for; matrix products, arithmetic and copies ran while one was open for 0% of the time, Pallas kernels for 21%

profile of v6, /device:TPU:448, one launch (start us, length us, event | category | flops | bytes accessed | tf_op | source)
XLA Modules:
  0.0 117.5 jit_solution(8428136278235467639)
XLA Ops:
  0.6 3.4 %collective-permute-start.1 = (bf16[768,768]{1,0:T(8,128)(2,1)}, bf16[768,768]{1,0:T(8,128)(2,1)S(1)}, u32[]{:S(2)}, u32[]{:S(2)}) collective-permute-start(bf16[768,768]{1,0:T(8,128)(2,1)} %bitcast.11), channel_id=1, source_target_pairs={{0,32},{16,48},{32,64},{48,80},{64,96},{80,112},{96,128},{112,144}... | collective-permute-start | bytes 3538952 | tf_op jit(solution)/shard_map/ppermute | solution.py:237
  4.0 3.1 %shard_map.77 = (f32[4,768]{1,0:T(4,128)}, f32[4,768]{1,0:T(4,128)}, f32[8,1,768]{2,1,0:T(1,128)}, bf16[800,256]{1,0:T(8,128)(2,1)}, bf16[800,256]{1,0:T(8,128)(2,1)}, /*index=5*/bf16[800,256]{1,0:T(8,128)(2,1)}) custom-call(s32[2,32]{1,0:T(2,128)} %plan_ref.1, f32[2,768]{1,0:T(2,128)} %bitcast.13, f32[2,768]{1,0:T(2,128)} %bitcast.14, f32[2,768]{1,0:T(2,128)} %bitcast.15, ...), custom_call_target="tpu_custom_call" | custom-call | tf_op jit(solution)/shard_map/pallas_call | solution.py:69
  7.1 4.5 %all-to-all-start = ((f32[8,1,768]{2,1,0:T(1,128)}), f32[8,1,768]{2,1,0:T(1,128)S(1)}, u32[]{:S(2)}, u32[]{:S(2)}) async-start(f32[8,1,768]{2,1,0:T(1,128)} %get-tuple-element.25), calls=%async_computation | async-start | bytes 49152 | tf_op jit(solution)/shard_map/all_to_all | solution.py:241
  11.7 1.9 %collective-permute-start = (f32[4,768]{1,0:T(4,128)}, f32[4,768]{1,0:T(4,128)S(1)}, u32[]{:S(2)}, u32[]{:S(2)}) collective-permute-start(f32[4,768]{1,0:T(4,128)} %get-tuple-element.26), channel_id=1, source_target_pairs={{0,16},{16,32},{32,48},{48,64},{64,80},{80,96},{96,112},{112,128},... | collective-permute-start | bytes 36872 | tf_op jit(solution)/shard_map/ppermute | solution.py:237
  13.6 3.2 %all-to-all-done = f32[8,1,768]{2,1,0:T(1,128)S(1)} async-done(((f32[8,1,768]{2,1,0:T(1,128)}), f32[8,1,768]{2,1,0:T(1,128)S(1)}, u32[]{:S(2)}, u32[]{:S(2)}) %all-to-all-start) | async-done | bytes 24608 | tf_op jit(solution)/shard_map/all_to_all | solution.py:241
  16.8 16.6 %psum.14.total_ref = f32[1,768]{1,0:T(1,128)} all-reduce(f32[1,768]{1,0:T(1,128)S(1)} %reduce_sum.23), channel_id=1, replica_groups=mesh['section'=32,'xh'=2,'z'=8] {'xh'}, use_global_device_ids=true, to_apply=%region_1.0 | all-reduce | flops 768 | bytes 6144 | tf_op jit(solution)/shard_map/psum | solution.py:241
  33.4 0.0 collective-permute-done.refs_1_
  33.4 1.4 %shard_map.78 = (f32[5,768]{1,0:T(8,128)}, bf16[800,256]{1,0:T(8,128)(2,1)}, bf16[800,256]{1,0:T(8,128)(2,1)}, bf16[800,256]{1,0:T(8,128)(2,1)}) custom-call(f32[1,768]{1,0:T(1,128)} %psum.14.total_ref, f32[4,768]{1,0:T(4,128)} %get-tuple-element.28.now_ref, ...), custom_call_target="tpu_custom_call", output_to_operand_aliasing={{1}: (2, {}), {2}: (3, {}), {3}: (4, {})} | custom-call | tf_op jit(solution)/shard_map/pallas_call | solution.py:103
  34.9 1.9 %collective-permute-start.2 = (f32[5,768]{1,0:T(8,128)}, f32[5,768]{1,0:T(8,128)S(1)}, u32[]{:S(2)}, u32[]{:S(2)}) collective-permute-start(f32[5,768]{1,0:T(8,128)} %get-tuple-element.35), channel_id=1, source_target_pairs={{0,32},{16,48},{32,64},{48,80},{64,96},{80,112},{96,128},{112,144}... | collective-permute-start | bytes 46088 | tf_op jit(solution)/shard_map/ppermute | solution.py:237
  36.8 6.1 %collective-permute-done.2.refs_0_.refs_1_ = f32[5,768]{1,0:T(8,128)S(1)} collective-permute-done((f32[5,768]{1,0:T(8,128)}, f32[5,768]{1,0:T(8,128)S(1)}, u32[]{:S(2)}, u32[]{:S(2)}) %collective-permute-start.2) | collective-permute-done | bytes 15392 | tf_op jit(solution)/shard_map/ppermute | solution.py:237
  42.9 0.0 collective-permute-done.1.x_ref
  42.9 0.0 copy-start
  42.9 1.0 copy-done
  43.9 7.7 %collective-permute-start.5 = (bf16[800,256]{1,0:T(8,128)(2,1)}, bf16[800,256]{1,0:T(8,128)(2,1)S(1)}, u32[]{:S(2)}, u32[]{:S(2)}) collective-permute-start(bf16[800,256]{1,0:T(8,128)(2,1)} %get-tuple-element.42), channel_id=1, source_target_pairs={{0,256},{16,272},{32,288},{48,304},{64,320},{80,336},{96,352},{112... | collective-permute-start | bytes 1228808 | tf_op jit(solution)/shard_map/ppermute | solution.py:237
  51.6 2.0 %collective-permute-start.4 = (bf16[800,256]{1,0:T(8,128)(2,1)}, bf16[800,256]{1,0:T(8,128)(2,1)S(1)}, u32[]{:S(2)}, u32[]{:S(2)}) collective-permute-start(bf16[800,256]{1,0:T(8,128)(2,1)} %get-tuple-element.41), channel_id=1, source_target_pairs={{0,256},{16,272},{32,288},{48,304},{64,320},{80,336},{96,352},{112... | collective-permute-start | bytes 1228808 | tf_op jit(solution)/shard_map/ppermute | solution.py:237
  53.7 7.7 %collective-permute-start.3 = (bf16[800,256]{1,0:T(8,128)(2,1)}, bf16[800,256]{1,0:T(8,128)(2,1)S(1)}, u32[]{:S(2)}, u32[]{:S(2)}) collective-permute-start(bf16[800,256]{1,0:T(8,128)(2,1)} %get-tuple-element.40), channel_id=1, source_target_pairs={{0,256},{16,272},{32,288},{48,304},{64,320},{80,336},{96,352},{112... | collective-permute-start | bytes 1228808 | tf_op jit(solution)/shard_map/ppermute | solution.py:237
  61.4 6.7 %shard_map.79 = (bf16[768,768]{1,0:T(8,128)(2,1)S(1)}, f32[8,1,768]{2,1,0:T(1,128)S(1)}) custom-call(bf16[768,768]{1,0:T(8,128)(2,1)} %copy-done, f32[5,768]{1,0:T(8,128)S(1)} %collective-permute-done.2.refs_0_.refs_1_, f32[5,768]{1,0:T(8,128)S(1)} %collective-permute-done.2.refs_0_.refs_1_), custom_call_target="tpu_custom_call" | custom-call | tf_op jit(solution)/shard_map/pallas_call | solution.py:201
  68.1 9.5 %all_to_all.10 = f32[8,1,768]{2,1,0:T(1,128)S(1)} all-to-all(f32[8,1,768]{2,1,0:T(1,128)S(1)} %get-tuple-element.39), channel_id=1, replica_groups=mesh['section'=32,'xh'=2,'z'=8] {'z'}, dimensions={0} | all-to-all | bytes 49152 | tf_op jit(solution)/shard_map/all_to_all | solution.py:241
  77.6 6.4 %psum.15.refs_0_ = f32[1,768]{1,0:T(1,128)S(1)} all-reduce(f32[1,768]{1,0:T(1,128)S(1)} %reduce_sum.25), channel_id=1, replica_groups=mesh['section'=32,'xh'=2,'z'=8] {'xh'}, use_global_device_ids=true, to_apply=%region_3.0 | all-reduce | flops 768 | bytes 6144 | tf_op jit(solution)/shard_map/psum | solution.py:241
  84.0 0.0 collective-permute-done.5.x_ref.refs_0_
  84.0 2.0 %shard_map.80 = bf16[768,256]{1,0:T(8,128)(2,1)S(1)} custom-call(bf16[800,256]{1,0:T(8,128)(2,1)S(1)} %collective-permute-done.5.x_ref.refs_0_), custom_call_target="tpu_custom_call" | custom-call | tf_op jit(solution)/shard_map/pallas_call | solution.py:201
  86.0 1.9 %collective-permute-start.6 = (bf16[768,256]{1,0:T(8,128)(2,1)S(1)}, bf16[768,256]{1,0:T(8,128)(2,1)S(1)}, u32[]{:S(2)}, u32[]{:S(2)}) collective-permute-start(bf16[768,256]{1,0:T(8,128)(2,1)S(1)} %shard_map.80), channel_id=1, source_target_pairs={{0,16},{16,32},{32,48},{48,64},{64,80},{80,96},{96,112},{112,128},... | collective-permute-start | bytes 1179656 | tf_op jit(solution)/shard_map/ppermute | solution.py:237
  87.9 9.0 %collective-permute-done.4.x_ref.refs_1_ = bf16[800,256]{1,0:T(8,128)(2,1)S(1)} collective-permute-done((bf16[800,256]{1,0:T(8,128)(2,1)}, bf16[800,256]{1,0:T(8,128)(2,1)S(1)}, u32[]{:S(2)}, u32[]{:S(2)}) %collective-permute-start.4) | collective-permute-done | bytes 409632 | tf_op jit(solution)/shard_map/ppermute | solution.py:237
  97.0 2.0 %shard_map.81 = bf16[768,256]{1,0:T(8,128)(2,1)S(1)} custom-call(bf16[800,256]{1,0:T(8,128)(2,1)S(1)} %collective-permute-done.4.x_ref.refs_1_), custom_call_target="tpu_custom_call" | custom-call | tf_op jit(solution)/shard_map/pallas_call | solution.py:201
  98.9 1.9 %collective-permute-start.7 = (bf16[768,256]{1,0:T(8,128)(2,1)S(1)}, bf16[768,256]{1,0:T(8,128)(2,1)S(1)}, u32[]{:S(2)}, u32[]{:S(2)}) collective-permute-start(bf16[768,256]{1,0:T(8,128)(2,1)S(1)} %shard_map.81), channel_id=1, source_target_pairs={{0,16},{16,32},{32,48},{48,64},{64,80},{80,96},{96,112},{112,128},... | collective-permute-start | bytes 1179656 | tf_op jit(solution)/shard_map/ppermute | solution.py:237
  100.8 2.7 %collective-permute-done.3.x_ref.refs_2_ = bf16[800,256]{1,0:T(8,128)(2,1)S(1)} collective-permute-done((bf16[800,256]{1,0:T(8,128)(2,1)}, bf16[800,256]{1,0:T(8,128)(2,1)S(1)}, u32[]{:S(2)}, u32[]{:S(2)}) %collective-permute-start.3) | collective-permute-done | bytes 409632 | tf_op jit(solution)/shard_map/ppermute | solution.py:237
  103.6 2.0 %shard_map.82 = bf16[768,256]{1,0:T(8,128)(2,1)S(1)} custom-call(bf16[800,256]{1,0:T(8,128)(2,1)S(1)} %collective-permute-done.3.x_ref.refs_2_), custom_call_target="tpu_custom_call" | custom-call | tf_op jit(solution)/shard_map/pallas_call | solution.py:201
  105.5 2.1 %collective-permute-start.8 = (bf16[768,256]{1,0:T(8,128)(2,1)S(1)}, bf16[768,256]{1,0:T(8,128)(2,1)S(1)}, u32[]{:S(2)}, u32[]{:S(2)}) collective-permute-start(bf16[768,256]{1,0:T(8,128)(2,1)S(1)} %shard_map.82), channel_id=1, source_target_pairs={{0,16},{16,32},{32,48},{48,64},{64,80},{80,96},{96,112},{112,128},... | collective-permute-start | bytes 1179656 | tf_op jit(solution)/shard_map/ppermute | solution.py:237
  107.6 5.6 %shard_map.83 = bf16[768,768]{1,0:T(8,128)(2,1)} custom-call(bf16[768,768]{1,0:T(8,128)(2,1)S(1)} %get-tuple-element.38.x_ref, f32[1,768]{1,0:T(1,128)S(1)} %psum.15.refs_0_, f32[4,768]{1,0:T(4,128)S(1)} %collective-permute-done.refs_1_), custom_call_target="tpu_custom_call" | custom-call | tf_op jit(solution)/shard_map/pallas_call | solution.py:201
  113.3 0.0 collective-permute-done.7.refs_4_
  113.3 0.0 collective-permute-done.6.refs_3_
  113.3 1.5 %shard_map.84 = bf16[2,768,768]{2,1,0:T(8,128)(2,1)} custom-call(bf16[800,256]{1,0:T(8,128)(2,1)S(1)} %collective-permute-done.5.x_ref.refs_0_, bf16[800,256]{1,0:T(8,128)(2,1)S(1)} %collective-permute-done.4.x_ref.refs_1_, bf16[800,256]{1,0:T(8,128)(2,1)S(1)} %collective-permute-done.3.x_ref.refs_2_, bf16[768,256]{1,0:T(8,128)(2,1)S(1)} %collective-permute-done.6.refs_3_, ...), custom_call_target="tpu_custom_call" | custom-call | tf_op jit(solution)/shard_map/pallas_call | solution.py:225
  114.8 1.9 %collective-permute-done.8 = bf16[768,256]{1,0:T(8,128)(2,1)S(1)} collective-permute-done((bf16[768,256]{1,0:T(8,128)(2,1)S(1)}, bf16[768,256]{1,0:T(8,128)(2,1)S(1)}, u32[]{:S(2)}, u32[]{:S(2)}) %collective-permute-start.8) | collective-permute-done | bytes 393248 | tf_op jit(solution)/shard_map/ppermute | solution.py:237
  116.7 0.8 bitcast_dynamic-update-slice_fusion
  (4 shorter events, 0.1 us)
Async XLA Ops:
  0.6 42.3 %collective-permute-start.1 = (bf16[768,768]{1,0:T(8,128)(2,1)}, bf16[768,768]{1,0:T(8,128)(2,1)S(1)}, u32[]{:S(2)}, u32[]{:S(2)}) collective-permute-start(bf16[768,768]{1,0:T(8,128)(2,1)} %bitcast.11), channel_id=1, source_target_pairs={{0,32},{16,48},{32,64},{48,80},{64,96},{80,112},{96,128},{112,144}... | collective-permute-start | bytes 3538952 | tf_op jit(solution)/shard_map/ppermute | solution.py:237
  7.1 9.6 %all-to-all-start = ((f32[8,1,768]{2,1,0:T(1,128)}), f32[8,1,768]{2,1,0:T(1,128)S(1)}, u32[]{:S(2)}, u32[]{:S(2)}) async-start(f32[8,1,768]{2,1,0:T(1,128)} %get-tuple-element.25), calls=%async_computation | async-start | bytes 49152 | tf_op jit(solution)/shard_map/all_to_all | solution.py:241
  11.7 21.8 %collective-permute-start = (f32[4,768]{1,0:T(4,128)}, f32[4,768]{1,0:T(4,128)S(1)}, u32[]{:S(2)}, u32[]{:S(2)}) collective-permute-start(f32[4,768]{1,0:T(4,128)} %get-tuple-element.26), channel_id=1, source_target_pairs={{0,16},{16,32},{32,48},{48,64},{64,80},{80,96},{96,112},{112,128},... | collective-permute-start | bytes 36872 | tf_op jit(solution)/shard_map/ppermute | solution.py:237
  34.9 8.0 %collective-permute-start.2 = (f32[5,768]{1,0:T(8,128)}, f32[5,768]{1,0:T(8,128)S(1)}, u32[]{:S(2)}, u32[]{:S(2)}) collective-permute-start(f32[5,768]{1,0:T(8,128)} %get-tuple-element.35), channel_id=1, source_target_pairs={{0,32},{16,48},{32,64},{48,80},{64,96},{80,112},{96,128},{112,144}... | collective-permute-start | bytes 46088 | tf_op jit(solution)/shard_map/ppermute | solution.py:237
  42.9 1.0 copy-start
  43.9 40.1 %collective-permute-start.5 = (bf16[800,256]{1,0:T(8,128)(2,1)}, bf16[800,256]{1,0:T(8,128)(2,1)S(1)}, u32[]{:S(2)}, u32[]{:S(2)}) collective-permute-start(bf16[800,256]{1,0:T(8,128)(2,1)} %get-tuple-element.42), channel_id=1, source_target_pairs={{0,256},{16,272},{32,288},{48,304},{64,320},{80,336},{96,352},{112... | collective-permute-start | bytes 1228808 | tf_op jit(solution)/shard_map/ppermute | solution.py:237
  51.6 45.3 %collective-permute-start.4 = (bf16[800,256]{1,0:T(8,128)(2,1)}, bf16[800,256]{1,0:T(8,128)(2,1)S(1)}, u32[]{:S(2)}, u32[]{:S(2)}) collective-permute-start(bf16[800,256]{1,0:T(8,128)(2,1)} %get-tuple-element.41), channel_id=1, source_target_pairs={{0,256},{16,272},{32,288},{48,304},{64,320},{80,336},{96,352},{112... | collective-permute-start | bytes 1228808 | tf_op jit(solution)/shard_map/ppermute | solution.py:237
  53.7 49.9 %collective-permute-start.3 = (bf16[800,256]{1,0:T(8,128)(2,1)}, bf16[800,256]{1,0:T(8,128)(2,1)S(1)}, u32[]{:S(2)}, u32[]{:S(2)}) collective-permute-start(bf16[800,256]{1,0:T(8,128)(2,1)} %get-tuple-element.40), channel_id=1, source_target_pairs={{0,256},{16,272},{32,288},{48,304},{64,320},{80,336},{96,352},{112... | collective-permute-start | bytes 1228808 | tf_op jit(solution)/shard_map/ppermute | solution.py:237
  86.0 27.3 %collective-permute-start.6 = (bf16[768,256]{1,0:T(8,128)(2,1)S(1)}, bf16[768,256]{1,0:T(8,128)(2,1)S(1)}, u32[]{:S(2)}, u32[]{:S(2)}) collective-permute-start(bf16[768,256]{1,0:T(8,128)(2,1)S(1)} %shard_map.80), channel_id=1, source_target_pairs={{0,16},{16,32},{32,48},{48,64},{64,80},{80,96},{96,112},{112,128},... | collective-permute-start | bytes 1179656 | tf_op jit(solution)/shard_map/ppermute | solution.py:237
  98.9 14.4 %collective-permute-start.7 = (bf16[768,256]{1,0:T(8,128)(2,1)S(1)}, bf16[768,256]{1,0:T(8,128)(2,1)S(1)}, u32[]{:S(2)}, u32[]{:S(2)}) collective-permute-start(bf16[768,256]{1,0:T(8,128)(2,1)S(1)} %shard_map.81), channel_id=1, source_target_pairs={{0,16},{16,32},{32,48},{48,64},{64,80},{80,96},{96,112},{112,128},... | collective-permute-start | bytes 1179656 | tf_op jit(solution)/shard_map/ppermute | solution.py:237
  105.5 11.2 %collective-permute-start.8 = (bf16[768,256]{1,0:T(8,128)(2,1)S(1)}, bf16[768,256]{1,0:T(8,128)(2,1)S(1)}, u32[]{:S(2)}, u32[]{:S(2)}) collective-permute-start(bf16[768,256]{1,0:T(8,128)(2,1)S(1)} %shard_map.82), channel_id=1, source_target_pairs={{0,16},{16,32},{32,48},{48,64},{64,80},{80,96},{96,112},{112,128},... | collective-permute-start | bytes 1179656 | tf_op jit(solution)/shard_map/ppermute | solution.py:237
